TPU v7x, 512 devices: a whole 4x4x16 slice. The times are simulated.
512 devices in a mesh: scen: 128 (over y, z_lo, x), dec: 4 (over z_hi, core).
Axes of the slice: x: 4, y: 4, z: 16 (z_hi: 2, z_lo: 8; z = z_hi * 8 + z_lo), core: 2. Of those that a mesh axis runs over, the one named last changes fastest.
Arguments:
- scen_duals: bfloat16 [32768, 1536], P('scen'), may hold values from -4.5 to 4.5
- recourse: bfloat16 [4, 1536, 4096], P(None, 'scen', 'dec'), may hold values from -0.15625 to 0.15625
- tile_active: int32 [32768, 12], P('scen'), may hold values 0 or 1
- scen_weights: float32 [32768], P('scen'), may hold values from 0.25 to 4
- cut_table: bfloat16 [2048, 8, 4096], P('scen', None, 'dec'), may hold values from -6 to 6
- cut_count: int32 [2048], P('scen'), may hold values from 0 to 7
- center: float32 [2048, 4096], P('scen', 'dec'), may hold values from -6 to 6
Outputs:
- node_means: float32 [4, 2048, 4096], P(None, 'scen', 'dec')
- new_cuts: bfloat16 [2048, 8, 4096], P('scen', None, 'dec')
- new_center: float32 [2048, 4096], P('scen', 'dec')
- scen_subgrads: bfloat16 [4, 32768, 4096], P(None, 'scen', 'dec')
All inputs are finite; a program needn't handle non-finite values. No bound on the sum of `tile_active` on one device may be relied on, other than what follows from the above.
Results may differ from a plain program's by a relative error of at most 0.001.
Values may be sent and summed in bfloat16 or wider, within the bound.
No kernel may reach another device: no remote copies, remote signals or barrier semaphores. Data moves between devices by JAX's collectives and lax.ppermute only.
A program may use at most 128 MiB of HBM per device.

v0:
```python
import jax
import jax.numpy as jnp
from jax import lax
from jax.sharding import PartitionSpec as P

LEAF = 16


step_size = 0.5


def local(scen_duals, recourse, tile_active, scen_weights, cut_table, cut_count, center):
    scen_count, row_count = scen_duals.shape
    tile_count = tile_active.shape[1]
    section_count = recourse.shape[0]
    local_cols = recourse.shape[2]
    masked = (
        scen_duals.reshape(scen_count, tile_count, row_count // tile_count)
        * tile_active.astype(jnp.bfloat16)[:, :, None]
    ).reshape(scen_count, row_count)
    subgrads = jnp.einsum(
        "sr,trd->tsd",
        masked,
        lax.all_gather(recourse, "scen", axis=1, tiled=True),
        preferred_element_type=jnp.float32,
    )
    scen_subgrads = subgrads.astype(jnp.bfloat16)
    weighted = subgrads * scen_weights[None, :, None]
    device_tot = jnp.sum(weighted[: section_count - 1], axis=1)
    device_w = jnp.sum(scen_weights)
    block_count = scen_count // LEAF
    leaf_sums = jnp.sum(weighted[section_count - 1].reshape(block_count, LEAF, local_cols), axis=1)
    leaf_w = jnp.sum(scen_weights.reshape(block_count, LEAF), axis=1)
    wide_count = lax.axis_size("scen")
    position = lax.axis_index("scen")
    group_mid = min(wide_count, LEAF * LEAF * LEAF // scen_count)
    mid_hot = (
        jnp.arange(wide_count // group_mid, dtype=jnp.int32) == position // group_mid
    ).astype(jnp.float32)
    table_parts = [device_tot[0][None], mid_hot[:, None] * device_tot[1][None]]
    weight_parts = [device_w[None], mid_hot * device_w]
    group_table = jnp.concatenate(table_parts, 0)
    weight_table = jnp.concatenate(weight_parts)
    summed, summed_w = lax.psum((group_table, weight_table), "scen")
    mid_row = 1 + position // group_mid
    row_picks = jnp.stack([jnp.zeros((), jnp.int32), mid_row])
    running = jnp.concatenate([jnp.take(summed, row_picks, axis=0), device_tot[2][None]], 0)
    run_weight = jnp.concatenate([jnp.take(summed_w, row_picks), device_w[None]])
    upper_means = running / run_weight[:, None]
    leaf_means = leaf_sums / leaf_w[:, None]
    node_means = jnp.concatenate(
        [
            jnp.broadcast_to(upper_means[:, None, :], (section_count - 1, block_count, local_cols)),
            leaf_means[None],
        ],
        0,
    )
    new_cut = leaf_means.astype(jnp.bfloat16)
    slot_ids = jnp.arange(cut_table.shape[1], dtype=jnp.int32)
    slot_hit = slot_ids[None, :] == cut_count[:, None]
    new_cuts = jnp.where(slot_hit[:, :, None], new_cut[:, None, :], cut_table)
    active_slot = slot_ids[None, :] <= cut_count[:, None]
    summed_cuts = jnp.sum(
        jnp.where(active_slot[:, :, None], new_cuts.astype(jnp.float32), 0.0), axis=1
    )
    aggregate = summed_cuts / (cut_count.astype(jnp.float32) + 1.0)[:, None]
    local_sq = jnp.sum(aggregate * aggregate, axis=1)
    total_sq = lax.psum(local_sq, "dec")
    scale_rms = jnp.sqrt(total_sq / (local_cols * lax.axis_size("dec")) + 1e-05)
    new_center = center - step_size * aggregate / scale_rms[:, None]
    return (node_means, new_cuts, new_center, scen_subgrads)


def solution(mesh):
    placed = (
        P("scen", None),
        P(None, "scen", "dec"),
        P("scen", None),
        P("scen"),
        P("scen", None, "dec"),
        P("scen"),
        P("scen", "dec"),
    )
    return jax.shard_map(
        local,
        mesh=mesh,
        in_specs=placed,
        out_specs=(
            P(None, "scen", "dec"),
            P("scen", None, "dec"),
            P("scen", "dec"),
            P(None, "scen", "dec"),
        ),
        check_vma=False,
    )
```

profile of v0, /device:TPU:1, one launch (start us, length us, event | category | flops | bytes accessed | tf_op | source)
XLA Modules:
  0.0 2073.7 jit_solution(2463932101728341027)
XLA Ops:
  7.2 0.0 all-gather.2.cloned.1.call-start
  7.2 0.7 all-gather.2.cloned.1.call-update
  7.9 1.4 copy.19
  9.3 0.7 convert_element_type.29
  10.0 0.8 reshape.217
  10.8 1.3 reduce_sum.57
  12.1 0.1 reduce_sum.60
  12.2 0.1 bitcast_multiply_fusion
  12.3 0.7 compare_select_fusion.2
  12.9 0.7 pad_maximum_fusion.2
  13.7 0.1 fusion.3
  13.7 0.7 convert_add_fusion
  14.4 0.7 iota_compare_fusion.1
  15.1 903.7 %all-gather.2.cloned.1.call-done = bf16[4,1536,1024]{2,0,1:T(4,128)(2,1)} async-done(((bf16[4,12,1024]{2,0,1:T(4,128)(2,1)}), bf16[4,1536,1024]{2,0,1:T(4,128)(2,1)}) %all-gather.2.cloned.1.call-update) | async-done | bytes 12582928 | tf_op jit(solution)/shard_map/all_gather | solution.py:24
  918.8 14.9 convert_bitcast_fusion
  933.7 0.0 copy-start
  933.7 0.0 copy-start.1
  933.7 0.1 slice.28
  933.8 0.2 slice_reduce_fusion
  934.0 0.2 reduce_sum.58
  934.2 0.1 bitcast_divide_fusion
  934.2 0.1 divide_convert_fusion
  934.3 0.1 broadcast_multiply_fusion
  934.4 919.2 %all-reduce = (f32[9,1024]{1,0:T(8,128)S(1)}, f32[9]{0:T(128)S(1)}) all-reduce(f32[9,1024]{1,0:T(8,128)S(1)} %pad_maximum_fusion.1, f32[9]{0:T(128)S(1)} %pad_maximum_fusion.2), channel_id=1, replica_groups=mesh['scen'=128,'dec'=4] {'scen'}, use_global_device_ids=true, to_apply=%region_1.0 | all-reduce | flops 9225 | bytes 73800 | tf_op jit(solution)/shard_map/psum | solution.py:44
  1853.7 0.6 gather_fusion
  1854.2 0.6 gather_fusion.1
  1854.9 0.1 broadcast_select_fusion.2
  1854.9 0.7 pad_maximum_fusion.3
  1855.7 0.0 copy-done
  1855.7 0.9 select_reduce_fusion
  1856.6 0.2 multiply_reduce_fusion
  1856.7 208.4 %psum.23 = f32[16]{0:T(128)S(1)} all-reduce(f32[16]{0:T(128)S(1)} %multiply_reduce_fusion), channel_id=1, replica_groups=mesh['scen'=128,'dec'=4] {'dec'}, use_global_device_ids=true, to_apply=%region_8.9 | all-reduce | flops 16 | bytes 128 | tf_op jit(solution)/shard_map/psum | solution.py:68
  2065.2 0.1 broadcast_select_fusion.1
  2065.3 0.1 maximum_divide_fusion
  2065.4 0.7 pad_maximum_fusion
  2066.1 0.0 copy-done.1
  2066.1 0.7 divide_subtract_fusion
  (6 shorter events, 0.1 us)
Async XLA Ops:
  7.2 911.7 %all-gather.2.cloned.1.call-start = ((), (), s32[]{:S(2)}) async-start(), calls=%async_computation | async-start | bytes 12681216 | tf_op jit(solution)/shard_map/all_gather | solution.py:24
  933.7 922.0 %copy-start = (bf16[16,8,1024]{2,1,0:T(8,128)(2,1)S(1)}, bf16[16,8,1024]{2,1,0:T(8,128)(2,1)}, u32[]{:S(2)}) copy-start(bf16[16,8,1024]{2,1,0:T(8,128)(2,1)} %param.11) | copy-start | bytes 786436
  933.7 1132.4 %copy-start.1 = (f32[16,1024]{1,0:T(8,128)S(1)}, f32[16,1024]{1,0:T(8,128)}, u32[]{:S(2)}) copy-start(f32[16,1024]{1,0:T(8,128)} %param.13) | copy-start | bytes 196612
Sparse Core Ops, SparseCore 0:
  10.1 908.7 all-gather.1
where the time goes:
time: 2070 us
  blocking collectives  1130 us (55%)
  waiting for transfers between devices  904 us (44%)
    psum x1, blocking collectives, local(): summed, summed_w = lax.psum((group_table, weight_table), 'scen')  919 us
    all_gather x1, waiting for transfers between devices, local(): lax.all_gather(recourse, 'scen', axis=1, tiled=True)  904 us
    psum x1, blocking collectives, local(): total_sq = lax.psum(local_sq, 'dec')  208 us
  transfers between devices with their start and end apart: 1, of which 1 were waited for; matrix products, arithmetic and copies ran while one was open for 0% of the time, Pallas kernels for 0%

commit v1 on v0

v1 whole, which is shorter than its diff:
```python
import jax
import jax.numpy as jnp
from jax import lax
from jax.sharding import Mesh
from jax.sharding import PartitionSpec as P

LEAF = 16
STEP = 0.5
F32 = jnp.float32
BF16 = jnp.bfloat16

NY, NQ, NR, NX = 4, 2, 4, 4
SCEN = ("y", "zq", "zr", "x")
DEC = ("zh", "c")


def exchange(value, axes):
    return lax.all_to_all(value, axes, 0, 0, tiled=True)


def spread(value, axes, count):
    return exchange(jnp.broadcast_to(value[None], (count,) + value.shape), axes)


def split_two(value):
    high = lax.reduce_precision(value, 8, 7)
    return high.astype(BF16), (value - high).astype(BF16)


def local(scen_duals, recourse, tile_active, scen_weights, cut_table, cut_count, center):
    rows, depth = scen_duals.shape
    tiles = tile_active.shape[1]
    sections, own_rows, cols = recourse.shape
    half = cols // 2
    blocks = rows // LEAF

    first = jnp.broadcast_to(recourse[None, :, :, :half], (NQ, NX, own_rows, half))
    first = exchange(first.reshape(NQ * NX, own_rows, half), ("zq", "x"))
    second = jnp.broadcast_to(recourse[:, None, :, half:], (NY, NQ, own_rows, half))
    second = exchange(second.reshape(NY * NQ, own_rows, half), ("y", "zq"))
    first = first.reshape(NQ, NX * own_rows, half)
    second = jnp.swapaxes(second.reshape(NY, NQ, own_rows, half), 0, 1).reshape(NQ, NY * own_rows, half)
    both = spread(jnp.stack([first, second]), "zr", NR)
    both = jnp.transpose(both, (1, 2, 0, 3, 4))
    first = spread(both[0], "y", NY).reshape(depth, half)
    second = spread(both[1], "x", NX).reshape(depth, half)

    masked = (
        scen_duals.reshape(rows, tiles, depth // tiles) * tile_active.astype(BF16)[:, :, None]
    ).reshape(rows, depth)
    weighted = masked.astype(F32) * scen_weights[:, None]
    leaf_v = jnp.sum(weighted.reshape(blocks, LEAF, depth), axis=1)
    leaf_w = jnp.sum(scen_weights.reshape(blocks, LEAF), axis=1)
    own_v = jnp.sum(leaf_v, axis=0)
    own_w = jnp.sum(leaf_w)
    leaf_hi, leaf_lo = split_two(leaf_v / leaf_w[:, None])
    own_hi, own_lo = split_two((own_v / own_w)[None])
    sums = jnp.concatenate([leaf_hi, leaf_lo, own_hi, own_lo, jnp.zeros((14, depth), BF16)], 0)
    packed = jnp.concatenate([masked, sums], 0)
    order = jnp.arange(depth, dtype=jnp.int32).reshape(NY, NQ * NR, NX, own_rows)
    order = jnp.transpose(order, (2, 1, 0, 3)).reshape(depth)
    one_hot = (jnp.arange(depth, dtype=jnp.int32)[:, None] == order[None, :]).astype(BF16)
    packed_y = jnp.dot(packed, one_hot, preferred_element_type=F32).astype(BF16)
    duals_x = spread(packed, "x", NX)
    duals_y = spread(packed_y, "y", NY)

    tree = jnp.concatenate([own_v, own_w[None], jnp.zeros((511,), F32)]).reshape(16, 128)
    mid = jnp.sum(spread(tree, ("zr", "x"), NR * NX), axis=0)
    mids = spread(mid, ("y", "zq"), NY * NQ).reshape(NY, NQ, 2048)
    root = jnp.sum(mids, axis=(0, 1))[None]
    mine = lax.dynamic_index_in_dim(mids, lax.axis_index("zq"), 1, keepdims=False)
    upper = jnp.concatenate([mine, root], 0)
    upper = upper[:, :depth] / upper[:, depth][:, None]
    upper_hi, upper_lo = split_two(upper)
    upper_rows = jnp.concatenate([upper_hi, upper_lo, jnp.zeros((6, depth), BF16)], 0)
    upper_rows_y = jnp.dot(upper_rows, one_hot, preferred_element_type=F32).astype(BF16)

    def node_part(duals, tops, rhs, axis):
        left = jnp.concatenate([duals[:, rows:].reshape(4 * 48, depth), tops], 0)
        got = jnp.dot(left, rhs, preferred_element_type=F32)
        low = got[: 4 * 48].reshape(4, 48, half)
        leaves = low[:, :16] + low[:, 16:32]
        owns = low[:, 32:33] + low[:, 33:34]
        top = got[4 * 48 : 4 * 48 + 5] + got[4 * 48 + 5 : 4 * 48 + 10]
        if axis == "x":
            middle = lax.dynamic_slice_in_dim(top, lax.axis_index("y"), 1, 0)
            middle = jnp.broadcast_to(middle[None], (4, 1, half))
        else:
            middle = top[:4, None]
        base = jnp.broadcast_to(top[4][None, None], (4, 1, half))
        send = jnp.concatenate([leaves, owns, middle, base, jnp.zeros((4, 5, half), F32)], 1)
        return exchange(send, axis)

    def grad_part(duals, rhs, axis):
        left = duals[:, :rows].reshape(4 * rows, depth)
        got = jnp.dot(left, rhs, preferred_element_type=F32).astype(BF16)
        return exchange(got.reshape(4, rows, half), axis)

    nodes_x = node_part(duals_x, upper_rows, first, "x")
    nodes_y = node_part(duals_y, upper_rows_y, second, "y")
    grads_x = grad_part(duals_x, first, "x")
    grads_y = grad_part(duals_y, second, "y")
    scen_subgrads = jnp.concatenate([grads_x, grads_y], -1)

    nodes = jnp.concatenate([nodes_x, nodes_y], -1)
    leaf_means = nodes[3, :16]
    uppers = jnp.stack([nodes[0, 18], nodes[1, 17], nodes[2, 16]])
    node_means = jnp.concatenate(
        [jnp.broadcast_to(uppers[:, None, :], (3, blocks, cols)), leaf_means[None]], 0
    )

    new_cut = leaf_means.astype(BF16)
    slot_ids = jnp.arange(cut_table.shape[1], dtype=jnp.int32)
    slot_hit = slot_ids[None, :] == cut_count[:, None]
    new_cuts = jnp.where(slot_hit[:, :, None], new_cut[:, None, :], cut_table)
    active = slot_ids[None, :] <= cut_count[:, None]
    total = jnp.sum(jnp.where(active[:, :, None], new_cuts.astype(F32), 0.0), axis=1)
    aggregate = total / (cut_count.astype(F32) + 1.0)[:, None]
    squares = jnp.sum(aggregate * aggregate, axis=1)
    total_sq = lax.psum(squares, DEC)
    scale = jnp.sqrt(total_sq / (cols * 4) + 1e-05)
    new_center = center - STEP * aggregate / scale[:, None]
    return (node_means, new_cuts, new_center, scen_subgrads)


def solution(mesh):
    fine = Mesh(mesh.devices.reshape(NY, NQ, NR, NX, 2, 2), SCEN + DEC)
    placed = (
        P(SCEN, None),
        P(None, SCEN, DEC),
        P(SCEN, None),
        P(SCEN),
        P(SCEN, None, DEC),
        P(SCEN),
        P(SCEN, DEC),
    )
    return jax.shard_map(
        local,
        mesh=fine,
        in_specs=placed,
        out_specs=(
            P(None, SCEN, DEC),
            P(SCEN, None, DEC),
            P(SCEN, DEC),
            P(None, SCEN, DEC),
        ),
        check_vma=False,
    )
```

time: 2070 us -> 316 us (0.15)
  the two profiles are of different devices: /device:TPU:1 before, /device:TPU:24 now
where the time goes in v1:
time: 316 us; the launch traced here: 314 us
  waiting for transfers between devices  157 us (50%)
  starting transfers between devices  71.2 us (23%)
  local copies, waits for them, and re-layouts  43.3 us (14%)
  matrix products  14.6 us (5%)
  blocking collectives  14.5 us (5%)
  other arithmetic  12 us (4%)
    all_to_all x13, waiting for transfers between devices, exchange(): return lax.all_to_all(value, axes, 0, 0, tiled=True)  157 us
    all_to_all x13, starting transfers between devices, exchange(): return lax.all_to_all(value, axes, 0, 0, tiled=True)  71.2 us
    psum x1, blocking collectives, local(): total_sq = lax.psum(squares, DEC)  14.5 us
    broadcast_in_dim x10, local copies, waits for them, and re-layouts, spread(): return exchange(jnp.broadcast_to(value[None], (count,) + value.shape), axes)  10.8 us
    dot_general x2, matrix products, grad_part(): got = jnp.dot(left, rhs, preferred_element_type=F32).astype(BF16)  8.33 us
  transfers between devices with their start and end apart: 13, of which 11 were waited for; matrix products, arithmetic and copies ran while one was open for 14% of the time, Pallas kernels for 0%

profile of v1, /device:TPU:24, one launch (start us, length us, event | category | flops | bytes accessed | tf_op | source)
XLA Modules:
  0.0 313.9 jit_solution(15571464202173600550)
XLA Ops:
  0.6 0.9 fusion.34
  1.5 0.7 broadcast_in_dim.154
  2.2 10.9 %all-to-all-start.3 = ((bf16[8,12,512]{2,1,0:T(8,128)(2,1)}), bf16[8,12,512]{2,1,0:T(8,128)(2,1)S(1)}, u32[]{:S(2)}, u32[]{:S(2)}) async-start(bf16[8,12,512]{2,1,0:T(8,128)(2,1)} %bitcast.6), calls=%async_computation.3 | async-start | bytes 262144 | tf_op jit(solution)/shard_map/all_to_all | solution.py:18
  13.1 0.7 convert_element_type.69
  13.8 1.4 copy.86
  16.4 0.7 concatenate.35
  17.1 8.6 %all-to-all-done.3 = bf16[8,12,512]{2,1,0:T(8,128)(2,1)S(1)} async-done(((bf16[8,12,512]{2,1,0:T(8,128)(2,1)}), bf16[8,12,512]{2,1,0:T(8,128)(2,1)S(1)}, u32[]{:S(2)}, u32[]{:S(2)}) %all-to-all-start.3) | async-done | bytes 98336 | tf_op jit(solution)/shard_map/all_to_all | solution.py:18
  25.6 0.7 broadcast_in_dim.79
  26.3 4.6 %all-to-all-start.1 = ((f32[16,16,128]{2,1,0:T(8,128)}), f32[16,16,128]{2,1,0:T(8,128)S(1)}, u32[]{:S(2)}, u32[]{:S(2)}) async-start(f32[16,16,128]{2,1,0:T(8,128)} %broadcast_in_dim.79), calls=%async_computation.1 | async-start | bytes 262144 | tf_op jit(solution)/shard_map/all_to_all | solution.py:18
  30.9 8.9 %all-to-all-done.1 = f32[16,16,128]{2,1,0:T(8,128)S(1)} async-done(((f32[16,16,128]{2,1,0:T(8,128)}), f32[16,16,128]{2,1,0:T(8,128)S(1)}, u32[]{:S(2)}, u32[]{:S(2)}) %all-to-all-start.1) | async-done | bytes 131104 | tf_op jit(solution)/shard_map/all_to_all | solution.py:18
  39.8 0.7 broadcast_in_dim.155
  40.5 6.5 %all-to-all-start.4 = ((bf16[8,12,512]{2,1,0:T(8,128)(2,1)}), bf16[8,12,512]{2,1,0:T(8,128)(2,1)S(1)}, u32[]{:S(2)}, u32[]{:S(2)}) async-start(bf16[8,12,512]{2,1,0:T(8,128)(2,1)} %bitcast.7), calls=%async_computation.4 | async-start | bytes 262144 | tf_op jit(solution)/shard_map/all_to_all | solution.py:18
  47.0 10.2 %all-to-all-done.4 = bf16[8,12,512]{2,1,0:T(8,128)(2,1)S(1)} async-done(((bf16[8,12,512]{2,1,0:T(8,128)(2,1)}), bf16[8,12,512]{2,1,0:T(8,128)(2,1)S(1)}, u32[]{:S(2)}, u32[]{:S(2)}) %all-to-all-start.4) | async-done | bytes 98336 | tf_op jit(solution)/shard_map/all_to_all | solution.py:18
  57.8 5.5 %all-to-all-start.2 = ((f32[8,16,128]{2,1,0:T(8,128)}), f32[8,16,128]{2,1,0:T(8,128)S(1)}, u32[]{:S(2)}, u32[]{:S(2)}) async-start(f32[8,16,128]{2,1,0:T(8,128)} %broadcast_in_dim.80), calls=%async_computation.2 | async-start | bytes 131072 | tf_op jit(solution)/shard_map/all_to_all | solution.py:18
  63.5 8.1 %all-to-all-done.2 = f32[8,16,128]{2,1,0:T(8,128)S(1)} async-done(((f32[8,16,128]{2,1,0:T(8,128)}), f32[8,16,128]{2,1,0:T(8,128)S(1)}, u32[]{:S(2)}, u32[]{:S(2)}) %all-to-all-start.2) | async-done | bytes 65568 | tf_op jit(solution)/shard_map/all_to_all | solution.py:18
  71.6 1.0 broadcast_in_dim.156
  72.6 4.2 %all-to-all-start.5 = ((bf16[4,2,2,48,512]{4,3,2,1,0:T(8,128)(2,1)}), bf16[4,2,2,48,512]{4,3,2,1,0:T(8,128)(2,1)}, u32[]{:S(2)}, u32[]{:S(2)}) async-start(bf16[4,2,2,48,512]{4,3,2,1,0:T(8,128)(2,1)} %broadcast_in_dim.156), calls=%async_computation.5 | async-start | bytes 1572864 | tf_op jit(solution)/shard_map/all_to_all | solution.py:18
  77.0 1.6 copy.87
  78.6 1.7 bitcast_reduce_fusion
  80.6 0.7 broadcast_divide_fusion.2
  82.1 0.8 broadcast_in_dim.74
  82.9 2.6 concatenate.34
  86.1 10.2 %all-to-all-done.5 = bf16[4,2,2,48,512]{4,3,2,1,0:T(8,128)(2,1)} async-done(((bf16[4,2,2,48,512]{4,3,2,1,0:T(8,128)(2,1)}), bf16[4,2,2,48,512]{4,3,2,1,0:T(8,128)(2,1)}, u32[]{:S(2)}, u32[]{:S(2)}) %all-to-all-start.5) | async-done | bytes 786464 | tf_op jit(solution)/shard_map/all_to_all | solution.py:18
  96.3 2.1 broadcast_in_dim.75
  98.5 4.8 %all-to-all-start = ((bf16[4,304,1536]{2,1,0:T(8,128)(2,1)}), bf16[4,304,1536]{2,1,0:T(8,128)(2,1)}, u32[]{:S(2)}, u32[]{:S(2)}) async-start(bf16[4,304,1536]{2,1,0:T(8,128)(2,1)} %broadcast_in_dim.75), calls=%async_computation | async-start | bytes 7471104 | tf_op jit(solution)/shard_map/all_to_all | solution.py:18
  103.4 1.9 fusion.4
  105.2 41.4 %all-to-all-done = bf16[4,304,1536]{2,1,0:T(8,128)(2,1)} async-done(((bf16[4,304,1536]{2,1,0:T(8,128)(2,1)}), bf16[4,304,1536]{2,1,0:T(8,128)(2,1)}, u32[]{:S(2)}, u32[]{:S(2)}) %all-to-all-start) | async-done | bytes 3735584 | tf_op jit(solution)/shard_map/all_to_all | solution.py:18
  146.6 2.3 broadcast_in_dim.163
  148.9 6.9 %all-to-all-start.8 = ((bf16[4,304,1536]{2,1,0:T(8,128)(2,1)}), bf16[4,304,1536]{2,1,0:T(8,128)(2,1)}, u32[]{:S(2)}, u32[]{:S(2)}) async-start(bf16[4,304,1536]{2,1,0:T(8,128)(2,1)} %broadcast_in_dim.163), calls=%async_computation.8 | async-start | bytes 7471104 | tf_op jit(solution)/shard_map/all_to_all | solution.py:18
  155.8 0.7 iota_compare_fusion.8
  156.5 1.2 slice_bitcast_fusion
  157.7 38.6 %all-to-all-done.8 = bf16[4,304,1536]{2,1,0:T(8,128)(2,1)} async-done(((bf16[4,304,1536]{2,1,0:T(8,128)(2,1)}), bf16[4,304,1536]{2,1,0:T(8,128)(2,1)}, u32[]{:S(2)}, u32[]{:S(2)}) %all-to-all-start.8) | async-done | bytes 3735584 | tf_op jit(solution)/shard_map/all_to_all | solution.py:18
  196.3 1.3 broadcast_in_dim.158
  197.6 5.7 %all-to-all-start.6 = ((bf16[4,2,4,48,512]{4,3,2,1,0:T(8,128)(2,1)}), bf16[4,2,4,48,512]{4,3,2,1,0:T(8,128)(2,1)S(1)}, u32[]{:S(2)}, u32[]{:S(2)}) async-start(bf16[4,2,4,48,512]{4,3,2,1,0:T(8,128)(2,1)} %broadcast_in_dim.158), calls=%async_computation.6 | async-start | bytes 3145728 | tf_op jit(solution)/shard_map/all_to_all | solution.py:18
  204.3 15.4 %all-to-all-done.6 = bf16[4,2,4,48,512]{4,3,2,1,0:T(8,128)(2,1)S(1)} async-done(((bf16[4,2,4,48,512]{4,3,2,1,0:T(8,128)(2,1)}), bf16[4,2,4,48,512]{4,3,2,1,0:T(8,128)(2,1)S(1)}, u32[]{:S(2)}, u32[]{:S(2)}) %all-to-all-start.6) | async-done | bytes 1572896 | tf_op jit(solution)/shard_map/all_to_all | solution.py:18
  219.7 1.5 broadcast_in_dim.165
  221.3 4.4 %all-to-all-start.9 = ((bf16[4,2,4,48,512]{4,3,2,1,0:T(8,128)(2,1)}), bf16[4,2,4,48,512]{4,3,2,1,0:T(8,128)(2,1)}, u32[]{:S(2)}, u32[]{:S(2)}) async-start(bf16[4,2,4,48,512]{4,3,2,1,0:T(8,128)(2,1)} %broadcast_in_dim.165), calls=%async_computation.9 | async-start | bytes 3145728 | tf_op jit(solution)/shard_map/all_to_all | solution.py:18
  225.7 1.7 fusion.5
  227.4 1.1 slice.124
  228.5 3.9 %slice.151 = bf16[4,256,1536]{2,1,0:T(8,128)(2,1)} slice(bf16[4,304,1536]{2,1,0:T(8,128)(2,1)} %all-to-all-done), slice={[0:4], [0:256], [0:1536]} | slice | bytes 6291456 | tf_op jit(solution)/shard_map/slice | solution.py:95
  232.4 1.9 slice.136
  234.3 2.2 slice.152
  237.8 0.7 slice_add_fusion.1
  238.5 4.7 %all-to-all-done.9 = bf16[4,2,4,48,512]{4,3,2,1,0:T(8,128)(2,1)} async-done(((bf16[4,2,4,48,512]{4,3,2,1,0:T(8,128)(2,1)}), bf16[4,2,4,48,512]{4,3,2,1,0:T(8,128)(2,1)}, u32[]{:S(2)}, u32[]{:S(2)}) %all-to-all-start.9) | async-done | bytes 1572896 | tf_op jit(solution)/shard_map/all_to_all | solution.py:18
  243.2 2.2 fusion.14
  246.6 4.2 %convolution_convert_fusion.1 = bf16[1024,512]{1,0:T(8,128)(2,1)} fusion(bf16[1024,1536]{1,0:T(8,128)(2,1)S(1)} %bitcast.54, bf16[1536,512]{1,0:T(8,128)(2,1)} %bitcast.55), kind=kOutput, calls=%fused_computation.11 | convolution fusion | flops 1611137024 | bytes 5767168 | tf_op jit(solution)/shard_map/dot_general | solution.py:96
  250.8 0.8 fusion.35
  252.8 3.1 concatenate.38
  255.9 4.0 %all-to-all-start.7 = ((f32[4,24,512]{2,1,0:T(8,128)}), f32[4,24,512]{2,1,0:T(8,128)}, u32[]{:S(2)}, u32[]{:S(2)}) async-start(f32[4,24,512]{2,1,0:T(8,128)} %concatenate.38), calls=%async_computation.7 | async-start | bytes 393216 | tf_op jit(solution)/shard_map/all_to_all | solution.py:18
  259.9 0.7 copy.100
  260.6 0.7 slice_add_fusion
  261.9 3.1 concatenate.41
  265.0 1.3 all-to-all-done.7
  266.3 5.4 %all-to-all-start.10 = ((f32[4,24,512]{2,1,0:T(8,128)}), f32[4,24,512]{2,1,0:T(8,128)S(1)}, u32[]{:S(2)}, u32[]{:S(2)}) async-start(f32[4,24,512]{2,1,0:T(8,128)} %concatenate.41), calls=%async_computation.10 | async-start | bytes 393216 | tf_op jit(solution)/shard_map/all_to_all | solution.py:18
  271.7 4.2 %convolution_convert_fusion = bf16[1024,512]{1,0:T(8,128)(2,1)} fusion(bf16[1024,1536]{1,0:T(8,128)(2,1)S(1)} %bitcast.53, bf16[1536,512]{1,0:T(8,128)(2,1)} %bitcast.20), kind=kOutput, calls=%fused_computation.10 | convolution fusion | flops 1611137024 | bytes 5767168 | tf_op jit(solution)/shard_map/dot_general | solution.py:96
  275.9 1.0 constant_dynamic-update-slice_fusion.1
  276.9 3.5 %all-to-all-start.11 = ((bf16[4,256,512]{2,1,0:T(8,128)(2,1)}), bf16[4,256,512]{2,1,0:T(8,128)(2,1)S(1)}, u32[]{:S(2)}, u32[]{:S(2)}) async-start(bf16[4,256,512]{2,1,0:T(8,128)(2,1)} %bitcast.61), calls=%async_computation.11 | async-start | bytes 2097152 | tf_op jit(solution)/shard_map/all_to_all | solution.py:18
  280.5 0.9 select_reduce_fusion
  281.4 9.8 %all-to-all-done.11 = bf16[4,256,512]{2,1,0:T(8,128)(2,1)S(1)} async-done(((bf16[4,256,512]{2,1,0:T(8,128)(2,1)}), bf16[4,256,512]{2,1,0:T(8,128)(2,1)S(1)}, u32[]{:S(2)}, u32[]{:S(2)}) %all-to-all-start.11) | async-done | bytes 1048608 | tf_op jit(solution)/shard_map/all_to_all | solution.py:18
  291.3 4.8 %all-to-all-start.12 = ((bf16[4,256,512]{2,1,0:T(8,128)(2,1)}), bf16[4,256,512]{2,1,0:T(8,128)(2,1)S(1)}, u32[]{:S(2)}, u32[]{:S(2)}) async-start(bf16[4,256,512]{2,1,0:T(8,128)(2,1)} %bitcast.31), calls=%async_computation.12 | async-start | bytes 2097152 | tf_op jit(solution)/shard_map/all_to_all | solution.py:18
  296.3 14.5 %psum.7 = f32[16]{0:T(128)S(1)} all-reduce(f32[16]{0:T(128)S(1)} %multiply_reduce_fusion), channel_id=1, replica_groups=mesh['y'=4,'zq'=2,'zr'=4,'x'=4,'zh'=2,'c'=2] {'zh','c'}, use_global_device_ids=true, to_apply=%region_8.9 | all-reduce | flops 16 | bytes 128 | tf_op jit(solution)/shard_map/psum | solution.py:120
  310.8 0.7 pad_maximum_fusion.1
  311.5 0.7 divide_subtract_fusion
  312.2 1.6 pad_maximum_fusion
  (81 shorter events, 9.6 us)
Async XLA Ops:
  0.6 14.6 %copy-start.7 = (f32[256]{0:T(256)S(1)}, f32[256]{0:T(256)}, u32[]{:S(2)}) copy-start(f32[256]{0:T(256)} %param.10) | copy-start | bytes 3076
  2.2 23.5 %all-to-all-start.3 = ((bf16[8,12,512]{2,1,0:T(8,128)(2,1)}), bf16[8,12,512]{2,1,0:T(8,128)(2,1)S(1)}, u32[]{:S(2)}, u32[]{:S(2)}) async-start(bf16[8,12,512]{2,1,0:T(8,128)(2,1)} %bitcast.6), calls=%async_computation.3 | async-start | bytes 262144 | tf_op jit(solution)/shard_map/all_to_all | solution.py:18
  26.3 13.5 %all-to-all-start.1 = ((f32[16,16,128]{2,1,0:T(8,128)}), f32[16,16,128]{2,1,0:T(8,128)S(1)}, u32[]{:S(2)}, u32[]{:S(2)}) async-start(f32[16,16,128]{2,1,0:T(8,128)} %broadcast_in_dim.79), calls=%async_computation.1 | async-start | bytes 262144 | tf_op jit(solution)/shard_map/all_to_all | solution.py:18
  40.5 16.7 %all-to-all-start.4 = ((bf16[8,12,512]{2,1,0:T(8,128)(2,1)}), bf16[8,12,512]{2,1,0:T(8,128)(2,1)S(1)}, u32[]{:S(2)}, u32[]{:S(2)}) async-start(bf16[8,12,512]{2,1,0:T(8,128)(2,1)} %bitcast.7), calls=%async_computation.4 | async-start | bytes 262144 | tf_op jit(solution)/shard_map/all_to_all | solution.py:18
  57.8 13.8 %all-to-all-start.2 = ((f32[8,16,128]{2,1,0:T(8,128)}), f32[8,16,128]{2,1,0:T(8,128)S(1)}, u32[]{:S(2)}, u32[]{:S(2)}) async-start(f32[8,16,128]{2,1,0:T(8,128)} %broadcast_in_dim.80), calls=%async_computation.2 | async-start | bytes 131072 | tf_op jit(solution)/shard_map/all_to_all | solution.py:18
  71.6 7.0 %copy-start.3 = (f32[8,16,128]{2,1,0:T(8,128)}, f32[8,16,128]{2,1,0:T(8,128)S(1)}, u32[]{:S(2)}) copy-start(f32[8,16,128]{2,1,0:T(8,128)S(1)} %all-to-all-done.2) | copy-start | bytes 196612
  72.6 23.7 %all-to-all-start.5 = ((bf16[4,2,2,48,512]{4,3,2,1,0:T(8,128)(2,1)}), bf16[4,2,2,48,512]{4,3,2,1,0:T(8,128)(2,1)}, u32[]{:S(2)}, u32[]{:S(2)}) async-start(bf16[4,2,2,48,512]{4,3,2,1,0:T(8,128)(2,1)} %broadcast_in_dim.156), calls=%async_computation.5 | async-start | bytes 1572864 | tf_op jit(solution)/shard_map/all_to_all | solution.py:18
  98.5 48.2 %all-to-all-start = ((bf16[4,304,1536]{2,1,0:T(8,128)(2,1)}), bf16[4,304,1536]{2,1,0:T(8,128)(2,1)}, u32[]{:S(2)}, u32[]{:S(2)}) async-start(bf16[4,304,1536]{2,1,0:T(8,128)(2,1)} %broadcast_in_dim.75), calls=%async_computation | async-start | bytes 7471104 | tf_op jit(solution)/shard_map/all_to_all | solution.py:18
  148.9 6.9 %copy-start.11 = (s32[16]{0:T(128)S(1)}, s32[16]{0:T(128)}, u32[]{:S(2)}) copy-start(s32[16]{0:T(128)} %param.12) | copy-start | bytes 196
  148.9 47.4 %all-to-all-start.8 = ((bf16[4,304,1536]{2,1,0:T(8,128)(2,1)}), bf16[4,304,1536]{2,1,0:T(8,128)(2,1)}, u32[]{:S(2)}, u32[]{:S(2)}) async-start(bf16[4,304,1536]{2,1,0:T(8,128)(2,1)} %broadcast_in_dim.163), calls=%async_computation.8 | async-start | bytes 7471104 | tf_op jit(solution)/shard_map/all_to_all | solution.py:18
  197.6 6.3 %copy-start.4 = (f32[8,16,128]{2,1,0:T(8,128)S(1)}, f32[8,16,128]{2,1,0:T(8,128)}, u32[]{:S(2)}) copy-start(f32[8,16,128]{2,1,0:T(8,128)} %copy-done.3) | copy-start | bytes 196612
  197.6 22.0 %all-to-all-start.6 = ((bf16[4,2,4,48,512]{4,3,2,1,0:T(8,128)(2,1)}), bf16[4,2,4,48,512]{4,3,2,1,0:T(8,128)(2,1)S(1)}, u32[]{:S(2)}, u32[]{:S(2)}) async-start(bf16[4,2,4,48,512]{4,3,2,1,0:T(8,128)(2,1)} %broadcast_in_dim.158), calls=%async_computation.6 | async-start | bytes 3145728 | tf_op jit(solution)/shard_map/all_to_all | solution.py:18
  219.7 1.7 copy-start.1
  221.3 21.9 %all-to-all-start.9 = ((bf16[4,2,4,48,512]{4,3,2,1,0:T(8,128)(2,1)}), bf16[4,2,4,48,512]{4,3,2,1,0:T(8,128)(2,1)}, u32[]{:S(2)}, u32[]{:S(2)}) async-start(bf16[4,2,4,48,512]{4,3,2,1,0:T(8,128)(2,1)} %broadcast_in_dim.165), calls=%async_computation.9 | async-start | bytes 3145728 | tf_op jit(solution)/shard_map/all_to_all | solution.py:18
  234.3 2.4 copy-start.2
  243.2 3.4 %copy-start = (bf16[4,256,1536]{2,1,0:T(8,128)(2,1)S(1)}, bf16[4,256,1536]{2,1,0:T(8,128)(2,1)}, u32[]{:S(2)}) copy-start(bf16[4,256,1536]{2,1,0:T(8,128)(2,1)} %slice.151) | copy-start | bytes 9437188
  255.9 10.4 %all-to-all-start.7 = ((f32[4,24,512]{2,1,0:T(8,128)}), f32[4,24,512]{2,1,0:T(8,128)}, u32[]{:S(2)}, u32[]{:S(2)}) async-start(f32[4,24,512]{2,1,0:T(8,128)} %concatenate.38), calls=%async_computation.7 | async-start | bytes 393216 | tf_op jit(solution)/shard_map/all_to_all | solution.py:18
  266.3 10.6 %all-to-all-start.10 = ((f32[4,24,512]{2,1,0:T(8,128)}), f32[4,24,512]{2,1,0:T(8,128)S(1)}, u32[]{:S(2)}, u32[]{:S(2)}) async-start(f32[4,24,512]{2,1,0:T(8,128)} %concatenate.41), calls=%async_computation.10 | async-start | bytes 393216 | tf_op jit(solution)/shard_map/all_to_all | solution.py:18
  275.9 4.6 %copy-start.5 = (bf16[16,8,1024]{2,1,0:T(8,128)(2,1)S(1)}, bf16[16,8,1024]{2,1,0:T(8,128)(2,1)}, u32[]{:S(2)}) copy-start(bf16[16,8,1024]{2,1,0:T(8,128)(2,1)} %param.11) | copy-start | bytes 786436
  275.9 4.6 %copy-start.8 = (pred[16,8]{1,0:T(8,128)(4,1)S(1)}, pred[16,8]{1,0:T(8,128)(4,1)}, u32[]{:S(2)}) copy-start(pred[16,8]{1,0:T(8,128)(4,1)} %get-tuple-element.23) | copy-start | bytes 388
  275.9 4.6 %copy-start.9 = (pred[16,8]{1,0:T(8,128)(4,1)S(1)}, pred[16,8]{1,0:T(8,128)(4,1)}, u32[]{:S(2)}) copy-start(pred[16,8]{1,0:T(8,128)(4,1)} %get-tuple-element.24) | copy-start | bytes 388
  276.9 14.4 %all-to-all-start.11 = ((bf16[4,256,512]{2,1,0:T(8,128)(2,1)}), bf16[4,256,512]{2,1,0:T(8,128)(2,1)S(1)}, u32[]{:S(2)}, u32[]{:S(2)}) async-start(bf16[4,256,512]{2,1,0:T(8,128)(2,1)} %bitcast.61), calls=%async_computation.11 | async-start | bytes 2097152 | tf_op jit(solution)/shard_map/all_to_all | solution.py:18
  280.4 15.6 %copy-start.10 = (f32[16]{0:T(128)S(1)}, f32[16]{0:T(128)}, u32[]{:S(2)}) copy-start(f32[16]{0:T(128)} %convert_add_fusion) | copy-start | bytes 196
  281.4 30.1 %copy-start.6 = (f32[16,1024]{1,0:T(8,128)S(1)}, f32[16,1024]{1,0:T(8,128)}, u32[]{:S(2)}) copy-start(f32[16,1024]{1,0:T(8,128)} %param.13) | copy-start | bytes 196612
  291.3 21.0 %all-to-all-start.12 = ((bf16[4,256,512]{2,1,0:T(8,128)(2,1)}), bf16[4,256,512]{2,1,0:T(8,128)(2,1)S(1)}, u32[]{:S(2)}, u32[]{:S(2)}) async-start(bf16[4,256,512]{2,1,0:T(8,128)(2,1)} %bitcast.31), calls=%async_computation.12 | async-start | bytes 2097152 | tf_op jit(solution)/shard_map/all_to_all | solution.py:18

commit v2 on v1

v2 whole, which is shorter than its diff:
```python
import jax
import jax.numpy as jnp
from jax import lax
from jax.experimental import pallas as pl
from jax.experimental.pallas import tpu as pltpu
from jax.sharding import Mesh
from jax.sharding import PartitionSpec as P

LEAF = 16
STEP = 0.5
F32 = jnp.float32
BF16 = jnp.bfloat16
VMEM_LIMIT = 48 * 1024 * 1024

NY, NQ, NR, NX = 4, 2, 4, 4
NZ = NQ * NR
SCEN = ("y", "zq", "zr", "x")
DEC = ("zh", "c")
EXTRA = 48
ARRIVED = (0, 4, 2, 6, 1, 5, 3, 7)


def exchange(value, axes):
    return lax.all_to_all(value, axes, 0, 0, tiled=True)


def spread(value, axes, count):
    return exchange(jnp.broadcast_to(value[None], (count,) + value.shape), axes)


def shift(value, axis, count, step):
    return lax.ppermute(value, axis, [((i + step) % count, i) for i in range(count)])


def flip(value, distance):
    return lax.ppermute(value, ("zq", "zr"), [(i, i ^ distance) for i in range(NZ)])


def split_two(value):
    high = value.astype(BF16)
    return high, (value - high.astype(F32)).astype(BF16)


def params(**more):
    return pltpu.CompilerParams(vmem_limit_bytes=VMEM_LIMIT, **more)


def cost(flops, size):
    return pl.CostEstimate(flops=flops, bytes_accessed=size, transcendentals=0)


def prepare_body(duals_ref, active_ref, weight_ref, packed_ref, tree_ref):
    rows, depth = duals_ref.shape
    tiles = active_ref.shape[1]
    width = depth // tiles
    blocks = rows // LEAF
    weight = weight_ref[...]
    leaf_w = jnp.sum(weight.reshape(blocks, LEAF, 1), axis=1)
    own_w = jnp.sum(leaf_w, axis=0, keepdims=True)
    active = active_ref[...].astype(F32)

    def put(at_rows, at, value):
        packed_ref[at_rows, at] = value

    for tile in range(tiles):
        at = slice(tile * width, (tile + 1) * width)
        masked = duals_ref[:, at].astype(F32) * active[:, tile : tile + 1]
        put(slice(EXTRA, None), at, masked.astype(BF16))
        leaf_v = jnp.sum((masked * weight).reshape(blocks, LEAF, width), axis=1)
        own_v = jnp.sum(leaf_v, axis=0, keepdims=True)
        high, low = split_two(leaf_v / leaf_w)
        put(slice(0, 16), at, high)
        put(slice(16, 32), at, low)
        high, low = split_two(jnp.broadcast_to(own_v / own_w, (8, width)))
        put(slice(32, 48), at, jnp.concatenate([high, low], 0))
        tree_ref[:, at] = own_v
    tree_ref[:, depth:] = jnp.broadcast_to(own_w, (1, 128))


def prepare(duals, active, weights):
    rows, depth = duals.shape
    return pl.pallas_call(
        prepare_body,
        out_shape=(
            jax.ShapeDtypeStruct((rows + EXTRA, depth), BF16),
            jax.ShapeDtypeStruct((1, depth + 128), F32),
        ),
        compiler_params=params(),
        cost_estimate=cost(4 * rows * depth, 4 * rows * depth),
    )(duals, active, weights[:, None])


def products_body(x_ref, y_ref, z_ref, top_ref, left_ref, *refs):
    pieces, (nodes_ref, grads_ref, rhs_ref) = refs[:10], refs[10:]
    block = rhs_ref.shape[0] // (NY * NZ)

    def put(step, offset, value):
        place = lax.rem(y_ref[0] + step, NY) * NZ + (z_ref[0] ^ offset)
        rhs_ref[pl.ds(pl.multiple_of(place * block, block), block)] = value

    for part in range(2):
        here, up, down, over, under = pieces[5 * part : 5 * part + 5]
        for index, offset in enumerate(ARRIVED[4 * part : 4 * part + 4]):
            at = slice(index * block, (index + 1) * block)
            put(0, offset, here[at])
            put(1, offset, up[at])
            put(3, offset, down[at])
            put(2, offset, (over[at] if index < 2 else under[(index - 2) * block : (index - 1) * block]))
    rhs = rhs_ref[...]
    cols = rhs.shape[1]
    rows = left_ref.shape[0] // NX
    top = jnp.dot(top_ref[...], rhs, preferred_element_type=F32)
    middle = top[0:1] + top[1:2]
    base = top[2:3] + top[3:4]
    row = lax.broadcasted_iota(jnp.int32, (8, cols), 0)
    whole = jnp.dot(left_ref[...], rhs, preferred_element_type=F32)
    for to in range(NX):
        got = whole[to * rows : (to + 1) * rows]
        grads_ref[to] = got[EXTRA:].astype(BF16)
        step = lax.rem(to - x_ref[0] + NX, NX)
        nodes_ref[step, 0:16] = got[0:16] + got[16:32]
        mean = got[32:33] + got[40:41]
        nodes_ref[step, 16:24] = jnp.where(row == 0, mean, jnp.where(row == 1, middle, base))


def products(x_at, y_at, z_at, top, left, pieces):
    rows, depth = left.shape
    rows = rows // NX - EXTRA
    cols = pieces[0].shape[1]
    steps = 4
    wide = cols // steps
    whole = lambda value: pl.BlockSpec(value.shape, lambda j: (0, 0))
    return pl.pallas_call(
        products_body,
        grid=(steps,),
        in_specs=[pl.BlockSpec(memory_space=pltpu.SMEM)] * 3
        + [whole(top), whole(left)]
        + [pl.BlockSpec((value.shape[0], wide), lambda j: (0, j)) for value in pieces],
        out_specs=(
            pl.BlockSpec((NX, 24, wide), lambda j: (0, 0, j)),
            pl.BlockSpec((NX, rows, wide), lambda j: (0, 0, j)),
        ),
        out_shape=(
            jax.ShapeDtypeStruct((NX, 24, cols), F32),
            jax.ShapeDtypeStruct((NX, rows, cols), BF16),
        ),
        scratch_shapes=[pltpu.VMEM((depth, wide), BF16)],
        compiler_params=params(),
        cost_estimate=cost(2 * NX * (rows + EXTRA) * depth * cols, 10_000_000),
    )(x_at, y_at, z_at, top, left, *pieces)


def local(scen_duals, recourse, tile_active, scen_weights, cut_table, cut_count, center):
    rows, depth = scen_duals.shape
    sections, own_rows, cols = recourse.shape
    blocks = rows // LEAF
    x_at = lax.axis_index("x")[None]
    y_at = lax.axis_index("y")[None]
    z_at = lax.axis_index(("zq", "zr"))[None]
    together = lax.optimization_barrier

    own = exchange(recourse, "x").reshape(1, NX * own_rows, cols)
    packed, tree = prepare(scen_duals, tile_active, scen_weights)
    own, tree = together((own, tree))
    far = flip(own, 4)
    left = lax.all_gather(packed, "x", axis=0, tiled=True)
    pair = jnp.concatenate([own, far], 0)
    four = jnp.concatenate([pair, flip(pair, 2)], 0)
    late = flip(four, 1)
    middle = jnp.sum(spread(tree, ("zr", "x"), NR * NX), axis=0)
    base = jnp.sum(spread(middle, ("y", "zq"), NY * NQ), axis=0)

    four = four.reshape(-1, cols)
    late = late.reshape(-1, cols)
    half = four.shape[0] // 2
    four_up = shift(four, "y", NY, 1)
    four_down = shift(four, "y", NY, 3)
    late_up = shift(late, "y", NY, 1)
    late_down = shift(late, "y", NY, 3)
    four_over = shift(four_up[:half], "y", NY, 1)
    four_under = shift(four_down[half:], "y", NY, 3)
    late_over = shift(late_up[:half], "y", NY, 1)
    late_under = shift(late_down[half:], "y", NY, 3)
    pieces = (four, four_up, four_down, four_over, four_under)
    pieces += (late, late_up, late_down, late_over, late_under)

    upper = jnp.concatenate([middle, base], 0)
    upper = upper[:, :depth] / upper[:, depth : depth + 1]
    first = lax.reduce_precision(upper, 8, 7)
    second = (upper - first).astype(BF16)
    first = first.astype(BF16)
    top = jnp.concatenate([first[:1], second[:1], first[1:], second[1:], jnp.zeros((12, depth), BF16)], 0)

    nodes, grads = products(x_at, y_at, z_at, top, left, pieces)
    sent = [nodes[0]] + [shift(nodes[step], "x", NX, NX - step) for step in (1, 2, 3)]
    scen_subgrads = exchange(grads, "x")
    line = jnp.stack(sent)

    def of_section(section):
        return lax.dynamic_index_in_dim(line, lax.rem(x_at[0] - section + NX, NX), 0, keepdims=False)

    leaf_means = of_section(3)[:16]
    uppers = jnp.stack([of_section(0)[18], of_section(1)[17], of_section(2)[16]])
    node_means = jnp.concatenate(
        [jnp.broadcast_to(uppers[:, None, :], (3, blocks, cols)), leaf_means[None]], 0
    )
    new_cut = leaf_means.astype(BF16)
    slot_ids = jnp.arange(cut_table.shape[1], dtype=jnp.int32)
    slot_hit = slot_ids[None, :] == cut_count[:, None]
    new_cuts = jnp.where(slot_hit[:, :, None], new_cut[:, None, :], cut_table)
    active = slot_ids[None, :] <= cut_count[:, None]
    total = jnp.sum(jnp.where(active[:, :, None], new_cuts.astype(F32), 0.0), axis=1)
    aggregate = total / (cut_count.astype(F32) + 1.0)[:, None]
    squares = jnp.sum(aggregate * aggregate, axis=1)
    total_sq = lax.psum(squares, DEC)
    scale = jnp.sqrt(total_sq / (cols * 4) + 1e-05)
    new_center = center - STEP * aggregate / scale[:, None]
    return (node_means, new_cuts, new_center, scen_subgrads)


def solution(mesh):
    fine = Mesh(mesh.devices.reshape(NY, NQ, NR, NX, 2, 2), SCEN + DEC)
    placed = (
        P(SCEN, None),
        P(None, SCEN, DEC),
        P(SCEN, None),
        P(SCEN),
        P(SCEN, None, DEC),
        P(SCEN),
        P(SCEN, DEC),
    )
    return jax.shard_map(
        local,
        mesh=fine,
        in_specs=placed,
        out_specs=(
            P(None, SCEN, DEC),
            P(SCEN, None, DEC),
            P(SCEN, DEC),
            P(None, SCEN, DEC),
        ),
        check_vma=False,
    )
```

time: 316 us -> 159 us (0.50)
  waiting for transfers between devices: 157 us -> 21.8 us
  local copies, waits for them, and re-layouts: 43.3 us -> 7.96 us
  matrix products: 14.6 us -> 0 us
  between operations: 1.09 us -> 14.5 us
  Pallas kernels: 0 us -> 10.5 us
  blocking collectives: 14.5 us -> 24.5 us
  other arithmetic: 12 us -> 3.05 us
  starting transfers between devices: 71.2 us -> 75.3 us
    all_to_all x13 -> x3, waiting for transfers between devices: 157 us -> 3.09 us  [exchange(): return lax.all_to_all(value, axes, 0, 0, tiled=True)]
    ppermute x0 -> x14, starting transfers between devices: none -> 55.1 us  [the longest x11 38.7 us: shift(): lax.ppermute(value, axis, [((i + step) % count, i) for i in range(count)])]
    all_to_all x13 -> x3, starting transfers between devices: 71.2 us -> 20.2 us  [exchange(): return lax.all_to_all(value, axes, 0, 0, tiled=True)]
    ppermute x0 -> x14, waiting for transfers between devices: none -> 18.7 us  [the longest x11 9.77 us: shift(): lax.ppermute(value, axis, [((i + step) % count, i) for i in range(count)])]
    dot_general x6 -> x0, matrix products: 14.6 us -> none  [the longest x2 8.33 us: grad_part(): got = jnp.dot(left, rhs, preferred_element_type=F32).astype(BF16)]
    pallas_call x0 -> x2, Pallas kernels: none -> 10.5 us  [the longest x1 8.81 us: products(): pl.pallas_call(products_body, grid=(steps,), in_specs=[pl.BlockSpec(memor...]
    all_to_all x0 -> x1, blocking collectives: none -> 10.1 us  [exchange(): return lax.all_to_all(value, axes, 0, 0, tiled=True)]
    concatenate x6 -> x2, local copies, waits for them, and re-layouts: 10.1 us -> 0.23 us  [the longest x1 0.22 us: local(): jnp.concatenate([first[:1], second[:1], first[1:], second[1:], jnp.zeros(...]
  transfers between devices with their start and end apart: 13 -> 18, of which waited for: 11 -> 7; matrix products, arithmetic and copies ran while one was open for 14% -> 4% of each run, Pallas kernels for 0% -> 0%
where the time goes in v2:
time: 159 us; the launch traced here: 158 us
  starting transfers between devices  75.3 us (47%)
  blocking collectives  24.5 us (15%)
  waiting for transfers between devices  21.8 us (14%)
  between operations  14.5 us (9%)
  Pallas kernels  10.5 us (7%)
  local copies, waits for them, and re-layouts  7.96 us (5%)
  other arithmetic  3.05 us (2%)
    ppermute x11, starting transfers between devices, shift(): lax.ppermute(value, axis, [((i + step) % count, i) for i in range(count)])  38.7 us
    all_to_all x3, starting transfers between devices, exchange(): return lax.all_to_all(value, axes, 0, 0, tiled=True)  20.2 us
    ppermute x3, starting transfers between devices, flip(): lax.ppermute(value, ('zq', 'zr'), [(i, i ^ distance) for i in range(NZ)])  16.4 us
    psum x1, blocking collectives, local(): total_sq = lax.psum(squares, DEC)  14.4 us
    all_to_all x1, blocking collectives, exchange(): return lax.all_to_all(value, axes, 0, 0, tiled=True)  10.1 us
    ppermute x11, waiting for transfers between devices, shift(): lax.ppermute(value, axis, [((i + step) % count, i) for i in range(count)])  9.77 us
    ppermute x3, waiting for transfers between devices, flip(): lax.ppermute(value, ('zq', 'zr'), [(i, i ^ distance) for i in range(NZ)])  8.96 us
    pallas_call x1, Pallas kernels, products(): pl.pallas_call(products_body, grid=(steps,), in_specs=[pl.BlockSpec(memor...  8.81 us
  transfers between devices with their start and end apart: 18, of which 7 were waited for; matrix products, arithmetic and copies ran while one was open for 4% of the time, Pallas kernels for 0%

profile of v2, /device:TPU:24, one launch (start us, length us, event | category | flops | bytes accessed | tf_op | source)
XLA Modules:
  0.0 157.7 jit_solution(12903764926626241234)
XLA Ops:
  7.2 0.0 copy-start.2
  7.2 0.0 copy-start.4
  7.2 0.0 all-gather.2.cloned.1.call-start
  7.2 0.8 copy.22.active_ref
  8.1 0.8 copy.23.weight_ref
  8.9 0.0 copy-start
  8.9 1.1 copy-done
  10.0 1.7 %shard_map.102 = (bf16[304,1536]{1,0:T(8,128)(2,1)}, f32[1,1664]{1,0:T(1,128)S(1)}) custom-call(bf16[256,1536]{1,0:T(8,128)(2,1)S(1)} %copy-done, s32[256,12]{1,0:T(8,128)S(1)} %copy.22.active_ref, f32[256,1]{1,0:T(8,128)S(1)} %copy.23.weight_ref), custom_call_target="tpu_custom_call" | custom-call | flops 1572864 | bytes 1572864 | tf_op jit(solution)/shard_map/pallas_call | solution.py:82
  11.7 0.0 all-gather.2.cloned.1.call-update
  11.7 0.0 copy-done.2
  11.8 10.1 %all_to_all.20 = bf16[4,12,1024]{2,1,0:T(8,128)(2,1)S(1)} all-to-all(bf16[4,12,1024]{2,1,0:T(8,128)(2,1)S(1)} %copy.21), channel_id=1, replica_groups=mesh['y'=4,'zq'=2,'zr'=4,'x'=4,'zh'=2,'c'=2] {'x'}, dimensions={0} | all-to-all | bytes 196608 | tf_op jit(solution)/shard_map/all_to_all | solution.py:24
  21.9 0.7 broadcast_in_dim.78
  22.6 6.6 %all-to-all-start.1 = ((f32[16,1,1664]{2,1,0:T(1,128)}), f32[16,1,1664]{2,1,0:T(1,128)S(1)}, u32[]{:S(2)}, u32[]{:S(2)}) async-start(f32[16,1,1664]{2,1,0:T(1,128)} %broadcast_in_dim.78), calls=%async_computation.1 | async-start | bytes 212992 | tf_op jit(solution)/shard_map/all_to_all | solution.py:24
  29.2 9.1 %collective-permute-start = (bf16[1,48,1024]{2,1,0:T(8,128)(2,1)S(1)}, bf16[1,48,1024]{2,1,0:T(8,128)(2,1)S(1)}, u32[]{:S(2)}, u32[]{:S(2)}) collective-permute-start(bf16[1,48,1024]{2,1,0:T(8,128)(2,1)S(1)} %reshape.80), channel_id=1, source_target_pairs={{0,64},{16,80},{32,96},{48,112},{64,0},{80,16},{96,32},{112,48},{1... | collective-permute-start | bytes 294920 | tf_op jit(solution)/shard_map/ppermute | solution.py:36
  38.4 0.1 iota_compare_fusion.1
  38.4 7.6 %collective-permute-done = bf16[1,48,1024]{2,1,0:T(8,128)(2,1)S(1)} collective-permute-done((bf16[1,48,1024]{2,1,0:T(8,128)(2,1)S(1)}, bf16[1,48,1024]{2,1,0:T(8,128)(2,1)S(1)}, u32[]{:S(2)}, u32[]{:S(2)}) %collective-permute-start) | collective-permute-done | bytes 98336 | tf_op jit(solution)/shard_map/ppermute | solution.py:36
  46.1 1.9 %collective-permute-start.1 = (bf16[2,48,1024]{2,1,0:T(8,128)(2,1)S(1)}, bf16[2,48,1024]{2,1,0:T(8,128)(2,1)S(1)}, u32[]{:S(2)}, u32[]{:S(2)}) collective-permute-start(bf16[2,48,1024]{2,1,0:T(8,128)(2,1)S(1)} %pad_maximum_fusion.2), channel_id=1, source_target_pairs={{0,32},{16,48},{32,0},{48,16},{64,96},{80,112},{96,64},{112,80},{1... | collective-permute-start | bytes 589832 | tf_op jit(solution)/shard_map/ppermute | solution.py:36
  48.0 0.0 all-to-all-done.1
  48.0 0.1 reduce_sum.40
  48.1 0.7 broadcast_in_dim.79
  48.8 9.8 %all-to-all-start.2 = ((f32[8,1,1664]{2,1,0:T(1,128)}), f32[8,1,1664]{2,1,0:T(1,128)S(1)}, u32[]{:S(2)}, u32[]{:S(2)}) async-start(f32[8,1,1664]{2,1,0:T(1,128)} %broadcast_in_dim.79), calls=%async_computation.2 | async-start | bytes 106496 | tf_op jit(solution)/shard_map/all_to_all | solution.py:24
  58.6 0.0 collective-permute-done.1
  58.6 5.4 %collective-permute-start.6 = (bf16[4,48,1024]{2,1,0:T(8,128)(2,1)S(1)}, bf16[4,48,1024]{2,1,0:T(8,128)(2,1)S(1)}, u32[]{:S(2)}, u32[]{:S(2)}) collective-permute-start(bf16[4,48,1024]{2,1,0:T(8,128)(2,1)S(1)} %constant_dynamic-update-slice_fusion), channel_id=1, source_target_pairs={{0,16},{16,0},{32,48},{48,32},{64,80},{80,64},{96,112},{112,96},{1... | collective-permute-start | bytes 1179656 | tf_op jit(solution)/shard_map/ppermute | solution.py:36
  64.0 2.8 %collective-permute-start.2 = (bf16[192,1024]{1,0:T(8,128)(2,1)S(1)}, bf16[192,1024]{1,0:T(8,128)(2,1)S(1)}, u32[]{:S(2)}, u32[]{:S(2)}) collective-permute-start(bf16[192,1024]{1,0:T(8,128)(2,1)S(1)} %bitcast.23), channel_id=1, source_target_pairs={{128,0},{256,128},{384,256},{0,384},{129,1},{257,129},{385,257},{1... | collective-permute-start | bytes 1179656 | tf_op jit(solution)/shard_map/ppermute | solution.py:32
  66.8 4.3 %collective-permute-start.3 = (bf16[192,1024]{1,0:T(8,128)(2,1)S(1)}, bf16[192,1024]{1,0:T(8,128)(2,1)S(1)}, u32[]{:S(2)}, u32[]{:S(2)}) collective-permute-start(bf16[192,1024]{1,0:T(8,128)(2,1)S(1)} %bitcast.24), channel_id=1, source_target_pairs={{384,0},{0,128},{128,256},{256,384},{385,1},{1,129},{129,257},{257... | collective-permute-start | bytes 1179656 | tf_op jit(solution)/shard_map/ppermute | solution.py:32
  71.1 0.0 all-to-all-done.2
  71.1 0.1 fusion.3
  71.3 0.1 fusion.2
  71.4 1.4 collective-permute-done.6
  72.7 2.2 %collective-permute-start.8 = (bf16[192,1024]{1,0:T(8,128)(2,1)S(1)}, bf16[192,1024]{1,0:T(8,128)(2,1)S(1)}, u32[]{:S(2)}, u32[]{:S(2)}) collective-permute-start(bf16[192,1024]{1,0:T(8,128)(2,1)S(1)} %bitcast.26), channel_id=1, source_target_pairs={{384,0},{0,128},{128,256},{256,384},{385,1},{1,129},{129,257},{257... | collective-permute-start | bytes 1179656 | tf_op jit(solution)/shard_map/ppermute | solution.py:32
  74.9 3.7 %collective-permute-start.7 = (bf16[192,1024]{1,0:T(8,128)(2,1)S(1)}, bf16[192,1024]{1,0:T(8,128)(2,1)S(1)}, u32[]{:S(2)}, u32[]{:S(2)}) collective-permute-start(bf16[192,1024]{1,0:T(8,128)(2,1)S(1)} %bitcast.27), channel_id=1, source_target_pairs={{128,0},{256,128},{384,256},{0,384},{129,1},{257,129},{385,257},{1... | collective-permute-start | bytes 1179656 | tf_op jit(solution)/shard_map/ppermute | solution.py:32
  78.6 0.0 collective-permute-done.2.refs_1_
  78.6 2.8 %collective-permute-start.4 = (bf16[96,1024]{1,0:T(8,128)(2,1)S(1)}, bf16[96,1024]{1,0:T(8,128)(2,1)S(1)}, u32[]{:S(2)}, u32[]{:S(2)}) collective-permute-start(bf16[96,1024]{1,0:T(8,128)(2,1)S(1)} %slice.91), channel_id=1, source_target_pairs={{128,0},{256,128},{384,256},{0,384},{129,1},{257,129},{385,257},{1... | collective-permute-start | bytes 589832 | tf_op jit(solution)/shard_map/ppermute | solution.py:32
  81.4 0.0 collective-permute-done.3.refs_2_
  81.4 0.7 slice.92
  82.1 4.8 %collective-permute-start.5 = (bf16[96,1024]{1,0:T(8,128)(2,1)}, bf16[96,1024]{1,0:T(8,128)(2,1)S(1)}, u32[]{:S(2)}, u32[]{:S(2)}) collective-permute-start(bf16[96,1024]{1,0:T(8,128)(2,1)} %slice.92), channel_id=1, source_target_pairs={{384,0},{0,128},{128,256},{256,384},{385,1},{1,129},{129,257},{257... | collective-permute-start | bytes 589832 | tf_op jit(solution)/shard_map/ppermute | solution.py:32
  86.9 1.9 %collective-permute-done.8.refs_7_ = bf16[192,1024]{1,0:T(8,128)(2,1)S(1)} collective-permute-done((bf16[192,1024]{1,0:T(8,128)(2,1)S(1)}, bf16[192,1024]{1,0:T(8,128)(2,1)S(1)}, u32[]{:S(2)}, u32[]{:S(2)}) %collective-permute-start.8) | collective-permute-done | bytes 393248 | tf_op jit(solution)/shard_map/ppermute | solution.py:32
  88.8 0.7 slice.94
  89.5 5.5 %collective-permute-start.10 = (bf16[96,1024]{1,0:T(8,128)(2,1)}, bf16[96,1024]{1,0:T(8,128)(2,1)S(1)}, u32[]{:S(2)}, u32[]{:S(2)}) collective-permute-start(bf16[96,1024]{1,0:T(8,128)(2,1)} %slice.94), channel_id=1, source_target_pairs={{384,0},{0,128},{128,256},{256,384},{385,1},{1,129},{129,257},{257... | collective-permute-start | bytes 589832 | tf_op jit(solution)/shard_map/ppermute | solution.py:32
  95.0 0.0 collective-permute-done.7.refs_6_
  95.0 0.7 slice.93
  95.7 1.9 %collective-permute-start.9 = (bf16[96,1024]{1,0:T(8,128)(2,1)}, bf16[96,1024]{1,0:T(8,128)(2,1)S(1)}, u32[]{:S(2)}, u32[]{:S(2)}) collective-permute-start(bf16[96,1024]{1,0:T(8,128)(2,1)} %slice.93), channel_id=1, source_target_pairs={{128,0},{256,128},{384,256},{0,384},{129,1},{257,129},{385,257},{1... | collective-permute-start | bytes 589832 | tf_op jit(solution)/shard_map/ppermute | solution.py:32
  97.7 0.2 concatenate.17.top_ref
  97.9 0.0 collective-permute-done.4.refs_3_
  97.9 0.0 collective-permute-done.5.refs_4_
  97.9 0.6 collective-permute-done.10.refs_9_
  98.5 6.2 %collective-permute-done.9.refs_8_ = bf16[96,1024]{1,0:T(8,128)(2,1)S(1)} collective-permute-done((bf16[96,1024]{1,0:T(8,128)(2,1)}, bf16[96,1024]{1,0:T(8,128)(2,1)S(1)}, u32[]{:S(2)}, u32[]{:S(2)}) %collective-permute-start.9) | collective-permute-done | bytes 196640 | tf_op jit(solution)/shard_map/ppermute | solution.py:32
  104.7 8.8 %shard_map.103 = (f32[4,24,1024]{2,1,0:T(8,128)S(1)}, bf16[4,256,1024]{2,1,0:T(8,128)(2,1)}) custom-call(s32[1]{0:T(128)} %bitcast.x_ref, s32[1]{0:T(128)} %bitcast.1.y_ref, s32[1]{0:T(128)} %bitcast.2.z_ref, bf16[16,1536]{1,0:T(8,128)(2,1)S(1)} %concatenate.17.top_ref, bf16[1216,1536]{1,0:T(8,128)(2,1)} %all-gather.2.cloned.1.call-done.left_ref, ...), custom_call_target="tpu_custom_call" | custom-call | flops 3825205248 | bytes 10000000 | tf_op jit(solution)/shard_map/pallas_call | solution.py:133
  113.5 4.8 %collective-permute-start.13 = (f32[24,1024]{1,0:T(8,128)S(1)}, f32[24,1024]{1,0:T(8,128)S(1)}, u32[]{:S(2)}, u32[]{:S(2)}) collective-permute-start(f32[24,1024]{1,0:T(8,128)S(1)} %get-tuple-element.26), channel_id=1, source_target_pairs={{4,0},{8,4},{12,8},{0,12},{5,1},{9,5},{13,9},{1,13},{6,2},{10,6},{... | collective-permute-start | bytes 294920 | tf_op jit(solution)/shard_map/ppermute | solution.py:32
  118.3 1.9 %collective-permute-start.11 = (f32[24,1024]{1,0:T(8,128)S(1)}, f32[24,1024]{1,0:T(8,128)S(1)}, u32[]{:S(2)}, u32[]{:S(2)}) collective-permute-start(f32[24,1024]{1,0:T(8,128)S(1)} %get-tuple-element.28), channel_id=1, source_target_pairs={{12,0},{0,4},{4,8},{8,12},{13,1},{1,5},{5,9},{9,13},{14,2},{2,6},{... | collective-permute-start | bytes 294920 | tf_op jit(solution)/shard_map/ppermute | solution.py:32
  120.2 4.2 %collective-permute-start.12 = (f32[24,1024]{1,0:T(8,128)S(1)}, f32[24,1024]{1,0:T(8,128)S(1)}, u32[]{:S(2)}, u32[]{:S(2)}) collective-permute-start(f32[24,1024]{1,0:T(8,128)S(1)} %get-tuple-element.27), channel_id=1, source_target_pairs={{8,0},{12,4},{0,8},{4,12},{9,1},{13,5},{1,9},{5,13},{10,2},{14,6},... | collective-permute-start | bytes 294920 | tf_op jit(solution)/shard_map/ppermute | solution.py:32
  124.5 0.0 copy-start.1
  124.5 3.8 %all-to-all-start.3 = ((bf16[4,256,1024]{2,1,0:T(8,128)(2,1)}), bf16[4,256,1024]{2,1,0:T(8,128)(2,1)S(1)}, u32[]{:S(2)}, u32[]{:S(2)}) async-start(bf16[4,256,1024]{2,1,0:T(8,128)(2,1)} %get-tuple-element.15), calls=%async_computation.3 | async-start | bytes 4194304 | tf_op jit(solution)/shard_map/all_to_all | solution.py:24
  128.2 0.0 copy-start.3
  128.3 0.0 collective-permute-done.13
  128.3 0.0 collective-permute-done.11
  128.3 1.1 collective-permute-done.12
  129.4 0.9 select_reduce_fusion
  130.3 0.2 multiply_reduce_fusion
  130.5 14.4 %psum.7 = f32[16]{0:T(128)S(1)} all-reduce(f32[16]{0:T(128)S(1)} %multiply_reduce_fusion), channel_id=1, replica_groups=mesh['y'=4,'zq'=2,'zr'=4,'x'=4,'zh'=2,'c'=2] {'zh','c'}, use_global_device_ids=true, to_apply=%region_4.5 | all-reduce | flops 16 | bytes 128 | tf_op jit(solution)/shard_map/psum | solution.py:215
  145.0 0.7 pad_maximum_fusion.1
  145.7 0.7 divide_subtract_fusion
  146.5 3.1 %all-to-all-done.3 = bf16[4,256,1024]{2,1,0:T(8,128)(2,1)S(1)} async-done(((bf16[4,256,1024]{2,1,0:T(8,128)(2,1)}), bf16[4,256,1024]{2,1,0:T(8,128)(2,1)S(1)}, u32[]{:S(2)}, u32[]{:S(2)}) %all-to-all-start.3) | async-done | bytes 2097184 | tf_op jit(solution)/shard_map/all_to_all | solution.py:24
  149.6 1.3 copy.31
  (26 shorter events, 0.4 us)
Async XLA Ops:
  7.2 4.6 %copy-start.2 = (bf16[4,12,1024]{2,0,1:T(4,128)(2,1)S(1)}, bf16[4,12,1024]{2,0,1:T(4,128)(2,1)}, u32[]{:S(2)}) copy-start(bf16[4,12,1024]{2,0,1:T(4,128)(2,1)} %param.8) | copy-start | bytes 294916
  7.2 31.2 %copy-start.4 = (s32[16]{0:T(128)S(1)}, s32[16]{0:T(128)}, u32[]{:S(2)}) copy-start(s32[16]{0:T(128)} %param.12) | copy-start | bytes 196
  7.2 97.5 %all-gather.2.cloned.1.call-start = ((), (), s32[]{:S(2)}) async-start(), calls=%async_computation.4 | async-start | bytes 4669440 | tf_op jit(solution)/shard_map/all_gather | solution.py:166
  8.9 1.1 copy-start
  22.6 25.4 %all-to-all-start.1 = ((f32[16,1,1664]{2,1,0:T(1,128)}), f32[16,1,1664]{2,1,0:T(1,128)S(1)}, u32[]{:S(2)}, u32[]{:S(2)}) async-start(f32[16,1,1664]{2,1,0:T(1,128)} %broadcast_in_dim.78), calls=%async_computation.1 | async-start | bytes 212992 | tf_op jit(solution)/shard_map/all_to_all | solution.py:24
  29.2 16.8 %collective-permute-start = (bf16[1,48,1024]{2,1,0:T(8,128)(2,1)S(1)}, bf16[1,48,1024]{2,1,0:T(8,128)(2,1)S(1)}, u32[]{:S(2)}, u32[]{:S(2)}) collective-permute-start(bf16[1,48,1024]{2,1,0:T(8,128)(2,1)S(1)} %reshape.80), channel_id=1, source_target_pairs={{0,64},{16,80},{32,96},{48,112},{64,0},{80,16},{96,32},{112,48},{1... | collective-permute-start | bytes 294920 | tf_op jit(solution)/shard_map/ppermute | solution.py:36
  46.1 12.5 %collective-permute-start.1 = (bf16[2,48,1024]{2,1,0:T(8,128)(2,1)S(1)}, bf16[2,48,1024]{2,1,0:T(8,128)(2,1)S(1)}, u32[]{:S(2)}, u32[]{:S(2)}) collective-permute-start(bf16[2,48,1024]{2,1,0:T(8,128)(2,1)S(1)} %pad_maximum_fusion.2), channel_id=1, source_target_pairs={{0,32},{16,48},{32,0},{48,16},{64,96},{80,112},{96,64},{112,80},{1... | collective-permute-start | bytes 589832 | tf_op jit(solution)/shard_map/ppermute | solution.py:36
  48.8 22.3 %all-to-all-start.2 = ((f32[8,1,1664]{2,1,0:T(1,128)}), f32[8,1,1664]{2,1,0:T(1,128)S(1)}, u32[]{:S(2)}, u32[]{:S(2)}) async-start(f32[8,1,1664]{2,1,0:T(1,128)} %broadcast_in_dim.79), calls=%async_computation.2 | async-start | bytes 106496 | tf_op jit(solution)/shard_map/all_to_all | solution.py:24
  58.6 14.1 %collective-permute-start.6 = (bf16[4,48,1024]{2,1,0:T(8,128)(2,1)S(1)}, bf16[4,48,1024]{2,1,0:T(8,128)(2,1)S(1)}, u32[]{:S(2)}, u32[]{:S(2)}) collective-permute-start(bf16[4,48,1024]{2,1,0:T(8,128)(2,1)S(1)} %constant_dynamic-update-slice_fusion), channel_id=1, source_target_pairs={{0,16},{16,0},{32,48},{48,32},{64,80},{80,64},{96,112},{112,96},{1... | collective-permute-start | bytes 1179656 | tf_op jit(solution)/shard_map/ppermute | solution.py:36
  64.0 14.6 %collective-permute-start.2 = (bf16[192,1024]{1,0:T(8,128)(2,1)S(1)}, bf16[192,1024]{1,0:T(8,128)(2,1)S(1)}, u32[]{:S(2)}, u32[]{:S(2)}) collective-permute-start(bf16[192,1024]{1,0:T(8,128)(2,1)S(1)} %bitcast.23), channel_id=1, source_target_pairs={{128,0},{256,128},{384,256},{0,384},{129,1},{257,129},{385,257},{1... | collective-permute-start | bytes 1179656 | tf_op jit(solution)/shard_map/ppermute | solution.py:32
  66.8 14.6 %collective-permute-start.3 = (bf16[192,1024]{1,0:T(8,128)(2,1)S(1)}, bf16[192,1024]{1,0:T(8,128)(2,1)S(1)}, u32[]{:S(2)}, u32[]{:S(2)}) collective-permute-start(bf16[192,1024]{1,0:T(8,128)(2,1)S(1)} %bitcast.24), channel_id=1, source_target_pairs={{384,0},{0,128},{128,256},{256,384},{385,1},{1,129},{129,257},{257... | collective-permute-start | bytes 1179656 | tf_op jit(solution)/shard_map/ppermute | solution.py:32
  72.7 16.1 %collective-permute-start.8 = (bf16[192,1024]{1,0:T(8,128)(2,1)S(1)}, bf16[192,1024]{1,0:T(8,128)(2,1)S(1)}, u32[]{:S(2)}, u32[]{:S(2)}) collective-permute-start(bf16[192,1024]{1,0:T(8,128)(2,1)S(1)} %bitcast.26), channel_id=1, source_target_pairs={{384,0},{0,128},{128,256},{256,384},{385,1},{1,129},{129,257},{257... | collective-permute-start | bytes 1179656 | tf_op jit(solution)/shard_map/ppermute | solution.py:32
  74.9 20.1 %collective-permute-start.7 = (bf16[192,1024]{1,0:T(8,128)(2,1)S(1)}, bf16[192,1024]{1,0:T(8,128)(2,1)S(1)}, u32[]{:S(2)}, u32[]{:S(2)}) collective-permute-start(bf16[192,1024]{1,0:T(8,128)(2,1)S(1)} %bitcast.27), channel_id=1, source_target_pairs={{128,0},{256,128},{384,256},{0,384},{129,1},{257,129},{385,257},{1... | collective-permute-start | bytes 1179656 | tf_op jit(solution)/shard_map/ppermute | solution.py:32
  78.6 19.3 %collective-permute-start.4 = (bf16[96,1024]{1,0:T(8,128)(2,1)S(1)}, bf16[96,1024]{1,0:T(8,128)(2,1)S(1)}, u32[]{:S(2)}, u32[]{:S(2)}) collective-permute-start(bf16[96,1024]{1,0:T(8,128)(2,1)S(1)} %slice.91), channel_id=1, source_target_pairs={{128,0},{256,128},{384,256},{0,384},{129,1},{257,129},{385,257},{1... | collective-permute-start | bytes 589832 | tf_op jit(solution)/shard_map/ppermute | solution.py:32
  82.1 15.8 %collective-permute-start.5 = (bf16[96,1024]{1,0:T(8,128)(2,1)}, bf16[96,1024]{1,0:T(8,128)(2,1)S(1)}, u32[]{:S(2)}, u32[]{:S(2)}) collective-permute-start(bf16[96,1024]{1,0:T(8,128)(2,1)} %slice.92), channel_id=1, source_target_pairs={{384,0},{0,128},{128,256},{256,384},{385,1},{1,129},{129,257},{257... | collective-permute-start | bytes 589832 | tf_op jit(solution)/shard_map/ppermute | solution.py:32
  89.5 9.0 %collective-permute-start.10 = (bf16[96,1024]{1,0:T(8,128)(2,1)}, bf16[96,1024]{1,0:T(8,128)(2,1)S(1)}, u32[]{:S(2)}, u32[]{:S(2)}) collective-permute-start(bf16[96,1024]{1,0:T(8,128)(2,1)} %slice.94), channel_id=1, source_target_pairs={{384,0},{0,128},{128,256},{256,384},{385,1},{1,129},{129,257},{257... | collective-permute-start | bytes 589832 | tf_op jit(solution)/shard_map/ppermute | solution.py:32
  95.7 9.0 %collective-permute-start.9 = (bf16[96,1024]{1,0:T(8,128)(2,1)}, bf16[96,1024]{1,0:T(8,128)(2,1)S(1)}, u32[]{:S(2)}, u32[]{:S(2)}) collective-permute-start(bf16[96,1024]{1,0:T(8,128)(2,1)} %slice.93), channel_id=1, source_target_pairs={{128,0},{256,128},{384,256},{0,384},{129,1},{257,129},{385,257},{1... | collective-permute-start | bytes 589832 | tf_op jit(solution)/shard_map/ppermute | solution.py:32
  113.5 14.7 %collective-permute-start.13 = (f32[24,1024]{1,0:T(8,128)S(1)}, f32[24,1024]{1,0:T(8,128)S(1)}, u32[]{:S(2)}, u32[]{:S(2)}) collective-permute-start(f32[24,1024]{1,0:T(8,128)S(1)} %get-tuple-element.26), channel_id=1, source_target_pairs={{4,0},{8,4},{12,8},{0,12},{5,1},{9,5},{13,9},{1,13},{6,2},{10,6},{... | collective-permute-start | bytes 294920 | tf_op jit(solution)/shard_map/ppermute | solution.py:32
  118.3 10.0 %collective-permute-start.11 = (f32[24,1024]{1,0:T(8,128)S(1)}, f32[24,1024]{1,0:T(8,128)S(1)}, u32[]{:S(2)}, u32[]{:S(2)}) collective-permute-start(f32[24,1024]{1,0:T(8,128)S(1)} %get-tuple-element.28), channel_id=1, source_target_pairs={{12,0},{0,4},{4,8},{8,12},{13,1},{1,5},{5,9},{9,13},{14,2},{2,6},{... | collective-permute-start | bytes 294920 | tf_op jit(solution)/shard_map/ppermute | solution.py:32
  120.2 9.1 %collective-permute-start.12 = (f32[24,1024]{1,0:T(8,128)S(1)}, f32[24,1024]{1,0:T(8,128)S(1)}, u32[]{:S(2)}, u32[]{:S(2)}) collective-permute-start(f32[24,1024]{1,0:T(8,128)S(1)} %get-tuple-element.27), channel_id=1, source_target_pairs={{8,0},{12,4},{0,8},{4,12},{9,1},{13,5},{1,9},{5,13},{10,2},{14,6},... | collective-permute-start | bytes 294920 | tf_op jit(solution)/shard_map/ppermute | solution.py:32
  124.5 5.0 %copy-start.1 = (bf16[16,8,1024]{2,1,0:T(8,128)(2,1)S(1)}, bf16[16,8,1024]{2,1,0:T(8,128)(2,1)}, u32[]{:S(2)}) copy-start(bf16[16,8,1024]{2,1,0:T(8,128)(2,1)} %param.11) | copy-start | bytes 786436
  124.5 25.1 %all-to-all-start.3 = ((bf16[4,256,1024]{2,1,0:T(8,128)(2,1)}), bf16[4,256,1024]{2,1,0:T(8,128)(2,1)S(1)}, u32[]{:S(2)}, u32[]{:S(2)}) async-start(bf16[4,256,1024]{2,1,0:T(8,128)(2,1)} %get-tuple-element.15), calls=%async_computation.3 | async-start | bytes 4194304 | tf_op jit(solution)/shard_map/all_to_all | solution.py:24
  128.2 17.5 %copy-start.3 = (f32[16,1024]{1,0:T(8,128)S(1)}, f32[16,1024]{1,0:T(8,128)}, u32[]{:S(2)}) copy-start(f32[16,1024]{1,0:T(8,128)} %param.13) | copy-start | bytes 196612
Sparse Core Ops, SparseCore 0:
  11.9 56.3 all-gather.1

commit v3 on v2

--- a/solution.py
+++ b/solution.py
@@ -49,45 +49,83 @@
     return pl.CostEstimate(flops=flops, bytes_accessed=size, transcendentals=0)
 
 
-def prepare_body(duals_ref, active_ref, weight_ref, packed_ref, tree_ref):
+def prepare_body(duals_ref, active_ref, weight_ref, recourse_ref, packed_ref, send_ref):
     rows, depth = duals_ref.shape
-    tiles = active_ref.shape[1]
+    tiles = active_ref.shape[0]
     width = depth // tiles
     blocks = rows // LEAF
-    weight = weight_ref[...]
+    cols = send_ref.shape[2]
+    weight = jnp.transpose(jnp.broadcast_to(weight_ref[...], (8, rows)))[:, :1]
     leaf_w = jnp.sum(weight.reshape(blocks, LEAF, 1), axis=1)
     own_w = jnp.sum(leaf_w, axis=0, keepdims=True)
-    active = active_ref[...].astype(F32)
-
-    def put(at_rows, at, value):
-        packed_ref[at_rows, at] = value
-
+    active = jnp.transpose(active_ref[...].astype(F32))
+    highs, lows = [], []
     for tile in range(tiles):
         at = slice(tile * width, (tile + 1) * width)
         masked = duals_ref[:, at].astype(F32) * active[:, tile : tile + 1]
-        put(slice(EXTRA, None), at, masked.astype(BF16))
+        packed_ref[EXTRA:, at] = masked.astype(BF16)
         leaf_v = jnp.sum((masked * weight).reshape(blocks, LEAF, width), axis=1)
         own_v = jnp.sum(leaf_v, axis=0, keepdims=True)
+        high, low = split_two(own_v)
+        highs.append(high.astype(F32))
+        lows.append(low.astype(F32))
         high, low = split_two(leaf_v / leaf_w)
-        put(slice(0, 16), at, high)
-        put(slice(16, 32), at, low)
+        packed_ref[:16, at] = high
+        packed_ref[16:32, at] = low
         high, low = split_two(jnp.broadcast_to(own_v / own_w, (8, width)))
-        put(slice(32, 48), at, jnp.concatenate([high, low], 0))
-        tree_ref[:, at] = own_v
-    tree_ref[:, depth:] = jnp.broadcast_to(own_w, (1, 128))
-
-
-def prepare(duals, active, weights):
+        packed_ref[32:48, at] = jnp.concatenate([high, low], 0)
+    high, low = jnp.concatenate(highs, 1), jnp.concatenate(lows, 1)
+    w_high, w_low = split_two(jnp.broadcast_to(own_w, (1, cols // 2)))
+    tree = jnp.concatenate(
+        [
+            high[:, :cols],
+            low[:, :cols],
+            jnp.concatenate([high[:, cols:], low[:, cols:]], 1),
+            jnp.concatenate([w_high.astype(F32), w_low.astype(F32)], 1),
+        ],
+        0,
+    )
+    for section in range(NX):
+        send_ref[section] = jnp.concatenate([recourse_ref[section].astype(F32), tree], 0).astype(BF16)
+
+
+def prepare(duals, active, weights, recourse):
     rows, depth = duals.shape
+    sections, own_rows, cols = recourse.shape
     return pl.pallas_call(
         prepare_body,
         out_shape=(
             jax.ShapeDtypeStruct((rows + EXTRA, depth), BF16),
-            jax.ShapeDtypeStruct((1, depth + 128), F32),
+            jax.ShapeDtypeStruct((NX, own_rows + 4, cols), BF16),
         ),
         compiler_params=params(),
         cost_estimate=cost(4 * rows * depth, 4 * rows * depth),
-    )(duals, active, weights[:, None])
+    )(duals, active.T, weights[None], recourse)
+
+
+def unpack_body(got_ref, slot_ref, tree_ref):
+    own_rows = got_ref.shape[1] - 4
+    cols = got_ref.shape[2]
+    extra = tree_ref.shape[1] - cols - 128
+    got = [got_ref[x].astype(F32) for x in range(NX)]
+    slot_ref[...] = jnp.concatenate([part[:own_rows] for part in got], 0).astype(BF16)
+    tree = sum(part[own_rows:] for part in got)
+    tree_ref[:, :cols] = tree[0:1] + tree[1:2]
+    tree_ref[:, cols : cols + extra] = tree[2:3, :extra] + tree[2:3, extra:]
+    tree_ref[:, cols + extra :] = tree[3:4, :128] + tree[3:4, cols // 2 : cols // 2 + 128]
+
+
+def unpack(got, depth):
+    _, rows, cols = got.shape
+    return pl.pallas_call(
+        unpack_body,
+        out_shape=(
+            jax.ShapeDtypeStruct((NX * (rows - 4), cols), BF16),
+            jax.ShapeDtypeStruct((1, depth + 128), F32),
+        ),
+        compiler_params=params(),
+        cost_estimate=cost(1000, 1000000),
+    )(got)
 
 
 def products_body(x_ref, y_ref, z_ref, top_ref, left_ref, *refs):
@@ -127,7 +165,7 @@
     rows, depth = left.shape
     rows = rows // NX - EXTRA
     cols = pieces[0].shape[1]
-    steps = 4
+    steps = 2
     wide = cols // steps
     whole = lambda value: pl.BlockSpec(value.shape, lambda j: (0, 0))
     return pl.pallas_call(
@@ -159,16 +197,16 @@
     z_at = lax.axis_index(("zq", "zr"))[None]
     together = lax.optimization_barrier
 
-    own = exchange(recourse, "x").reshape(1, NX * own_rows, cols)
-    packed, tree = prepare(scen_duals, tile_active, scen_weights)
-    own, tree = together((own, tree))
+    packed, send = prepare(scen_duals, tile_active, scen_weights, recourse)
+    own, tree = unpack(exchange(send, "x"), depth)
+    own = own[None]
+    left = lax.all_gather(packed, "x", axis=0, tiled=True)
     far = flip(own, 4)
-    left = lax.all_gather(packed, "x", axis=0, tiled=True)
     pair = jnp.concatenate([own, far], 0)
     four = jnp.concatenate([pair, flip(pair, 2)], 0)
     late = flip(four, 1)
-    middle = jnp.sum(spread(tree, ("zr", "x"), NR * NX), axis=0)
-    base = jnp.sum(spread(middle, ("y", "zq"), NY * NQ), axis=0)
+    row = jnp.sum(spread(tree, "y", NY), axis=0)
+    trees = spread(jnp.concatenate([tree, row], 0), ("zq", "zr"), NZ)
 
     four = four.reshape(-1, cols)
     late = late.reshape(-1, cols)
@@ -184,6 +222,9 @@
     pieces = (four, four_up, four_down, four_over, four_under)
     pieces += (late, late_up, late_down, late_over, late_under)
 
+    trees = jnp.sum(trees.reshape(NQ, NR, 2, depth + 128), axis=1)
+    middle = lax.dynamic_index_in_dim(trees[:, 0], lax.axis_index("zq"), 0)
+    base = jnp.sum(trees[:, 1], axis=0, keepdims=True)
     upper = jnp.concatenate([middle, base], 0)
     upper = upper[:, :depth] / upper[:, depth : depth + 1]
     first = lax.reduce_precision(upper, 8, 7)

time: 159 us -> 155 us (0.975)
  starting transfers between devices: 75.3 us -> 68.4 us
  blocking collectives: 24.5 us -> 30.4 us
  waiting for transfers between devices: 21.8 us -> 19 us
    psum x1, blocking collectives: 14.4 us -> 20.3 us  [local(): total_sq = lax.psum(squares, DEC)]
    ppermute x3, starting transfers between devices: 16.4 us -> 12.9 us  [flip(): lax.ppermute(value, ('zq', 'zr'), [(i, i ^ distance) for i in range(NZ)])]
    all_to_all x3, waiting for transfers between devices: 3.09 us -> 0.01 us  [exchange(): return lax.all_to_all(value, axes, 0, 0, tiled=True)]
    all_to_all x3, starting transfers between devices: 20.2 us -> 18.1 us  [exchange(): return lax.all_to_all(value, axes, 0, 0, tiled=True)]
    unnamed x15 -> x14, local copies, waits for them, and re-layouts: 3.35 us -> 4.78 us
  transfers between devices with their start and end apart: 18 -> 18, of which waited for: 7 -> 8; matrix products, arithmetic and copies ran while one was open for 4% -> 4% of each run, Pallas kernels for 0% -> 0%
where the time goes in v3:
time: 155 us; the launch traced here: 154 us
  starting transfers between devices  68.4 us (44%)
  blocking collectives  30.4 us (20%)
  waiting for transfers between devices  19 us (12%)
  between operations  14.4 us (9%)
  Pallas kernels  10.1 us (7%)
  local copies, waits for them, and re-layouts  8.51 us (5%)
  other arithmetic  3.09 us (2%)
    ppermute x11, starting transfers between devices, shift(): lax.ppermute(value, axis, [((i + step) % count, i) for i in range(count)])  37.4 us
    psum x1, blocking collectives, local(): total_sq = lax.psum(squares, DEC)  20.3 us
    all_to_all x3, starting transfers between devices, exchange(): return lax.all_to_all(value, axes, 0, 0, tiled=True)  18.1 us
    ppermute x3, starting transfers between devices, flip(): lax.ppermute(value, ('zq', 'zr'), [(i, i ^ distance) for i in range(NZ)])  12.9 us
    ppermute x3, waiting for transfers between devices, flip(): lax.ppermute(value, ('zq', 'zr'), [(i, i ^ distance) for i in range(NZ)])  10.1 us
    all_to_all x1, blocking collectives, exchange(): return lax.all_to_all(value, axes, 0, 0, tiled=True)  10.1 us
    ppermute x11, waiting for transfers between devices, shift(): lax.ppermute(value, axis, [((i + step) % count, i) for i in range(count)])  8.84 us
    pallas_call x1, Pallas kernels, products(): pl.pallas_call(products_body, grid=(steps,), in_specs=[pl.BlockSpec(memor...  8.18 us
  transfers between devices with their start and end apart: 18, of which 8 were waited for; matrix products, arithmetic and copies ran while one was open for 4% of the time, Pallas kernels for 0%

profile of v3, /device:TPU:24, one launch (start us, length us, event | category | flops | bytes accessed | tf_op | source)
XLA Modules:
  0.0 153.9 jit_solution(2431968715123559839)
XLA Ops:
  7.2 0.0 copy-start.5
  7.2 0.0 all-gather.2.cloned.1.call-start
  7.2 0.9 copy.18.recourse_ref
  8.2 0.0 copy-start
  8.2 1.1 copy-done
  9.3 0.7 copy-done.1
  10.0 0.7 copy-done.2
  10.7 1.8 %shard_map.102 = (bf16[304,1536]{1,0:T(8,128)(2,1)}, bf16[4,16,1024]{2,1,0:T(8,128)(2,1)S(1)}) custom-call(bf16[256,1536]{1,0:T(8,128)(2,1)S(1)} %copy-done, s32[12,256]{1,0:T(8,128)S(1)} %bitcast.35, f32[1,256]{1,0:T(1,128)S(1)} %bitcast.36, bf16[4,12,1024]{2,1,0:T(8,128)(2,1)S(1)} %copy.18.recourse_ref), custom_call_target="tpu_custom_call" | custom-call | flops 1572864 | bytes 1572864 | tf_op jit(solution)/shard_map/pallas_call | solution.py:95
  12.5 0.0 all-gather.2.cloned.1.call-update
  12.6 10.1 %all_to_all.20.got_ref = bf16[4,16,1024]{2,1,0:T(8,128)(2,1)S(1)} all-to-all(bf16[4,16,1024]{2,1,0:T(8,128)(2,1)S(1)} %get-tuple-element.10), channel_id=1, replica_groups=mesh['y'=4,'zq'=2,'zr'=4,'x'=4,'zh'=2,'c'=2] {'x'}, dimensions={0} | all-to-all | bytes 262144 | tf_op jit(solution)/shard_map/all_to_all | solution.py:24
  22.7 0.6 broadcast_in_dim.84
  23.3 7.1 %all-to-all-start.1 = ((f32[4,1,1664]{2,1,0:T(1,128)}), f32[4,1,1664]{2,1,0:T(1,128)S(1)}, u32[]{:S(2)}, u32[]{:S(2)}) async-start(f32[4,1,1664]{2,1,0:T(1,128)} %broadcast_in_dim.84), calls=%async_computation.1 | async-start | bytes 53248 | tf_op jit(solution)/shard_map/all_to_all | solution.py:24
  30.4 6.6 %collective-permute-start = (bf16[1,48,1024]{2,1,0:T(8,128)(2,1)S(1)}, bf16[1,48,1024]{2,1,0:T(8,128)(2,1)S(1)}, u32[]{:S(2)}, u32[]{:S(2)}) collective-permute-start(bf16[1,48,1024]{2,1,0:T(8,128)(2,1)S(1)} %bitcast.32), channel_id=1, source_target_pairs={{0,64},{16,80},{32,96},{48,112},{64,0},{80,16},{96,32},{112,48},{1... | collective-permute-start | bytes 294920 | tf_op jit(solution)/shard_map/ppermute | solution.py:36
  37.1 0.0 all-to-all-done.1
  37.2 0.7 broadcast_in_dim.85
  37.9 6.8 %all-to-all-start.2 = ((f32[8,2,1664]{2,1,0:T(2,128)}), f32[8,2,1664]{2,1,0:T(2,128)S(1)}, u32[]{:S(2)}, u32[]{:S(2)}) async-start(f32[8,2,1664]{2,1,0:T(2,128)} %broadcast_in_dim.85), calls=%async_computation.2 | async-start | bytes 212992 | tf_op jit(solution)/shard_map/all_to_all | solution.py:24
  44.6 0.5 collective-permute-done
  45.2 4.3 %collective-permute-start.1 = (bf16[2,48,1024]{2,1,0:T(8,128)(2,1)S(1)}, bf16[2,48,1024]{2,1,0:T(8,128)(2,1)S(1)}, u32[]{:S(2)}, u32[]{:S(2)}) collective-permute-start(bf16[2,48,1024]{2,1,0:T(8,128)(2,1)S(1)} %pad_maximum_fusion.3), channel_id=1, source_target_pairs={{0,32},{16,48},{32,0},{48,16},{64,96},{80,112},{96,64},{112,80},{1... | collective-permute-start | bytes 589832 | tf_op jit(solution)/shard_map/ppermute | solution.py:36
  49.5 0.0 copy-done.5
  49.5 0.1 iota_compare_fusion.1
  49.6 9.3 %collective-permute-done.1 = bf16[2,48,1024]{2,1,0:T(8,128)(2,1)S(1)} collective-permute-done((bf16[2,48,1024]{2,1,0:T(8,128)(2,1)S(1)}, bf16[2,48,1024]{2,1,0:T(8,128)(2,1)S(1)}, u32[]{:S(2)}, u32[]{:S(2)}) %collective-permute-start.1) | collective-permute-done | bytes 196640 | tf_op jit(solution)/shard_map/ppermute | solution.py:36
  58.9 1.9 %collective-permute-start.6 = (bf16[4,48,1024]{2,1,0:T(8,128)(2,1)S(1)}, bf16[4,48,1024]{2,1,0:T(8,128)(2,1)S(1)}, u32[]{:S(2)}, u32[]{:S(2)}) collective-permute-start(bf16[4,48,1024]{2,1,0:T(8,128)(2,1)S(1)} %pad_maximum_fusion), channel_id=1, source_target_pairs={{0,16},{16,0},{32,48},{48,32},{64,80},{80,64},{96,112},{112,96},{1... | collective-permute-start | bytes 1179656 | tf_op jit(solution)/shard_map/ppermute | solution.py:36
  60.8 2.6 %collective-permute-start.2 = (bf16[192,1024]{1,0:T(8,128)(2,1)S(1)}, bf16[192,1024]{1,0:T(8,128)(2,1)S(1)}, u32[]{:S(2)}, u32[]{:S(2)}) collective-permute-start(bf16[192,1024]{1,0:T(8,128)(2,1)S(1)} %bitcast.29), channel_id=1, source_target_pairs={{128,0},{256,128},{384,256},{0,384},{129,1},{257,129},{385,257},{1... | collective-permute-start | bytes 1179656 | tf_op jit(solution)/shard_map/ppermute | solution.py:32
  63.4 4.4 %collective-permute-start.3 = (bf16[192,1024]{1,0:T(8,128)(2,1)S(1)}, bf16[192,1024]{1,0:T(8,128)(2,1)S(1)}, u32[]{:S(2)}, u32[]{:S(2)}) collective-permute-start(bf16[192,1024]{1,0:T(8,128)(2,1)S(1)} %bitcast.30), channel_id=1, source_target_pairs={{384,0},{0,128},{128,256},{256,384},{385,1},{1,129},{129,257},{257... | collective-permute-start | bytes 1179656 | tf_op jit(solution)/shard_map/ppermute | solution.py:32
  67.9 0.0 all-to-all-done.2
  68.0 0.1 fusion.3
  68.1 0.1 fusion.2
  68.2 0.3 collective-permute-done.6
  68.5 4.4 %collective-permute-start.8 = (bf16[192,1024]{1,0:T(8,128)(2,1)S(1)}, bf16[192,1024]{1,0:T(8,128)(2,1)S(1)}, u32[]{:S(2)}, u32[]{:S(2)}) collective-permute-start(bf16[192,1024]{1,0:T(8,128)(2,1)S(1)} %bitcast.37), channel_id=1, source_target_pairs={{384,0},{0,128},{128,256},{256,384},{385,1},{1,129},{129,257},{257... | collective-permute-start | bytes 1179656 | tf_op jit(solution)/shard_map/ppermute | solution.py:32
  72.9 1.9 %collective-permute-start.7 = (bf16[192,1024]{1,0:T(8,128)(2,1)S(1)}, bf16[192,1024]{1,0:T(8,128)(2,1)S(1)}, u32[]{:S(2)}, u32[]{:S(2)}) collective-permute-start(bf16[192,1024]{1,0:T(8,128)(2,1)S(1)} %bitcast.38), channel_id=1, source_target_pairs={{128,0},{256,128},{384,256},{0,384},{129,1},{257,129},{385,257},{1... | collective-permute-start | bytes 1179656 | tf_op jit(solution)/shard_map/ppermute | solution.py:32
  74.9 0.0 collective-permute-done.2.refs_1_
  74.9 2.1 %collective-permute-start.4 = (bf16[96,1024]{1,0:T(8,128)(2,1)S(1)}, bf16[96,1024]{1,0:T(8,128)(2,1)S(1)}, u32[]{:S(2)}, u32[]{:S(2)}) collective-permute-start(bf16[96,1024]{1,0:T(8,128)(2,1)S(1)} %slice.101), channel_id=1, source_target_pairs={{128,0},{256,128},{384,256},{0,384},{129,1},{257,129},{385,257},{1... | collective-permute-start | bytes 589832 | tf_op jit(solution)/shard_map/ppermute | solution.py:32
  77.1 0.4 collective-permute-done.3.refs_2_
  77.4 0.7 slice.102
  78.1 5.6 %collective-permute-start.5 = (bf16[96,1024]{1,0:T(8,128)(2,1)}, bf16[96,1024]{1,0:T(8,128)(2,1)S(1)}, u32[]{:S(2)}, u32[]{:S(2)}) collective-permute-start(bf16[96,1024]{1,0:T(8,128)(2,1)} %slice.102), channel_id=1, source_target_pairs={{384,0},{0,128},{128,256},{256,384},{385,1},{1,129},{129,257},{257... | collective-permute-start | bytes 589832 | tf_op jit(solution)/shard_map/ppermute | solution.py:32
  83.7 1.0 collective-permute-done.8.refs_7_
  84.7 0.7 slice.104
  85.4 5.4 %collective-permute-start.10 = (bf16[96,1024]{1,0:T(8,128)(2,1)}, bf16[96,1024]{1,0:T(8,128)(2,1)S(1)}, u32[]{:S(2)}, u32[]{:S(2)}) collective-permute-start(bf16[96,1024]{1,0:T(8,128)(2,1)} %slice.104), channel_id=1, source_target_pairs={{384,0},{0,128},{128,256},{256,384},{385,1},{1,129},{129,257},{257... | collective-permute-start | bytes 589832 | tf_op jit(solution)/shard_map/ppermute | solution.py:32
  90.8 0.0 collective-permute-done.7.refs_6_
  90.8 0.7 slice.103
  91.5 1.9 %collective-permute-start.9 = (bf16[96,1024]{1,0:T(8,128)(2,1)}, bf16[96,1024]{1,0:T(8,128)(2,1)S(1)}, u32[]{:S(2)}, u32[]{:S(2)}) collective-permute-start(bf16[96,1024]{1,0:T(8,128)(2,1)} %slice.103), channel_id=1, source_target_pairs={{128,0},{256,128},{384,256},{0,384},{129,1},{257,129},{385,257},{1... | collective-permute-start | bytes 589832 | tf_op jit(solution)/shard_map/ppermute | solution.py:32
  93.4 0.2 concatenate.21.top_ref
  93.6 0.0 collective-permute-done.4.refs_3_
  93.6 0.0 collective-permute-done.5.refs_4_
  93.7 0.6 collective-permute-done.10.refs_9_
  94.2 6.2 %collective-permute-done.9.refs_8_ = bf16[96,1024]{1,0:T(8,128)(2,1)S(1)} collective-permute-done((bf16[96,1024]{1,0:T(8,128)(2,1)}, bf16[96,1024]{1,0:T(8,128)(2,1)S(1)}, u32[]{:S(2)}, u32[]{:S(2)}) %collective-permute-start.9) | collective-permute-done | bytes 196640 | tf_op jit(solution)/shard_map/ppermute | solution.py:32
  100.4 8.2 %shard_map.104 = (f32[4,24,1024]{2,1,0:T(8,128)S(1)}, bf16[4,256,1024]{2,1,0:T(8,128)(2,1)}) custom-call(s32[1]{0:T(128)} %bitcast.x_ref, s32[1]{0:T(128)} %bitcast.1.y_ref, s32[1]{0:T(128)} %bitcast.2.z_ref, bf16[16,1536]{1,0:T(8,128)(2,1)S(1)} %concatenate.21.top_ref, bf16[1216,1536]{1,0:T(8,128)(2,1)} %all-gather.2.cloned.1.call-done.left_ref, ...), custom_call_target="tpu_custom_call" | custom-call | flops 3825205248 | bytes 10000000 | tf_op jit(solution)/shard_map/pallas_call | solution.py:171
  108.6 2.4 %collective-permute-start.11 = (f32[24,1024]{1,0:T(8,128)S(1)}, f32[24,1024]{1,0:T(8,128)S(1)}, u32[]{:S(2)}, u32[]{:S(2)}) collective-permute-start(f32[24,1024]{1,0:T(8,128)S(1)} %get-tuple-element.28), channel_id=1, source_target_pairs={{12,0},{0,4},{4,8},{8,12},{13,1},{1,5},{5,9},{9,13},{14,2},{2,6},{... | collective-permute-start | bytes 294920 | tf_op jit(solution)/shard_map/ppermute | solution.py:32
  111.0 4.1 %collective-permute-start.12 = (f32[24,1024]{1,0:T(8,128)S(1)}, f32[24,1024]{1,0:T(8,128)S(1)}, u32[]{:S(2)}, u32[]{:S(2)}) collective-permute-start(f32[24,1024]{1,0:T(8,128)S(1)} %get-tuple-element.27), channel_id=1, source_target_pairs={{8,0},{12,4},{0,8},{4,12},{9,1},{13,5},{1,9},{5,13},{10,2},{14,6},... | collective-permute-start | bytes 294920 | tf_op jit(solution)/shard_map/ppermute | solution.py:32
  115.1 2.6 %collective-permute-start.13 = (f32[24,1024]{1,0:T(8,128)S(1)}, f32[24,1024]{1,0:T(8,128)S(1)}, u32[]{:S(2)}, u32[]{:S(2)}) collective-permute-start(f32[24,1024]{1,0:T(8,128)S(1)} %get-tuple-element.26), channel_id=1, source_target_pairs={{4,0},{8,4},{12,8},{0,12},{5,1},{9,5},{13,9},{1,13},{6,2},{10,6},{... | collective-permute-start | bytes 294920 | tf_op jit(solution)/shard_map/ppermute | solution.py:32
  117.7 0.0 copy-start.3
  117.7 4.2 %all-to-all-start.3 = ((bf16[4,256,1024]{2,1,0:T(8,128)(2,1)}), bf16[4,256,1024]{2,1,0:T(8,128)(2,1)S(1)}, u32[]{:S(2)}, u32[]{:S(2)}) async-start(bf16[4,256,1024]{2,1,0:T(8,128)(2,1)} %get-tuple-element.15), calls=%async_computation.3 | async-start | bytes 4194304 | tf_op jit(solution)/shard_map/all_to_all | solution.py:24
  122.0 0.0 collective-permute-done.11
  122.0 0.0 collective-permute-done.12
  122.0 0.7 collective-permute-done.13
  122.8 0.0 copy-done.3
  122.8 0.9 select_reduce_fusion
  123.7 0.2 multiply_reduce_fusion
  123.9 20.3 %psum.7 = f32[16]{0:T(128)S(1)} all-reduce(f32[16]{0:T(128)S(1)} %multiply_reduce_fusion), channel_id=1, replica_groups=mesh['y'=4,'zq'=2,'zr'=4,'x'=4,'zh'=2,'c'=2] {'zh','c'}, use_global_device_ids=true, to_apply=%region_5.6 | all-reduce | flops 16 | bytes 128 | tf_op jit(solution)/shard_map/psum | solution.py:256
  144.3 0.7 pad_maximum_fusion.2
  145.0 0.0 copy-done.4
  145.0 0.7 divide_subtract_fusion
  145.7 0.0 all-to-all-done.3
  145.7 1.3 copy.29
  (27 shorter events, 0.4 us)
Async XLA Ops:
  7.2 42.3 %copy-start.5 = (s32[16]{0:T(128)S(1)}, s32[16]{0:T(128)}, u32[]{:S(2)}) copy-start(s32[16]{0:T(128)} %param.12) | copy-start | bytes 196
  7.2 93.3 %all-gather.2.cloned.1.call-start = ((), (), s32[]{:S(2)}) async-start(), calls=%async_computation.4 | async-start | bytes 4669440 | tf_op jit(solution)/shard_map/all_gather | solution.py:203
  8.2 1.1 copy-start
  9.3 0.7 copy-start.1
  10.0 0.7 copy-start.2
  23.3 13.8 %all-to-all-start.1 = ((f32[4,1,1664]{2,1,0:T(1,128)}), f32[4,1,1664]{2,1,0:T(1,128)S(1)}, u32[]{:S(2)}, u32[]{:S(2)}) async-start(f32[4,1,1664]{2,1,0:T(1,128)} %broadcast_in_dim.84), calls=%async_computation.1 | async-start | bytes 53248 | tf_op jit(solution)/shard_map/all_to_all | solution.py:24
  30.4 14.7 %collective-permute-start = (bf16[1,48,1024]{2,1,0:T(8,128)(2,1)S(1)}, bf16[1,48,1024]{2,1,0:T(8,128)(2,1)S(1)}, u32[]{:S(2)}, u32[]{:S(2)}) collective-permute-start(bf16[1,48,1024]{2,1,0:T(8,128)(2,1)S(1)} %bitcast.32), channel_id=1, source_target_pairs={{0,64},{16,80},{32,96},{48,112},{64,0},{80,16},{96,32},{112,48},{1... | collective-permute-start | bytes 294920 | tf_op jit(solution)/shard_map/ppermute | solution.py:36
  37.9 30.0 %all-to-all-start.2 = ((f32[8,2,1664]{2,1,0:T(2,128)}), f32[8,2,1664]{2,1,0:T(2,128)S(1)}, u32[]{:S(2)}, u32[]{:S(2)}) async-start(f32[8,2,1664]{2,1,0:T(2,128)} %broadcast_in_dim.85), calls=%async_computation.2 | async-start | bytes 212992 | tf_op jit(solution)/shard_map/all_to_all | solution.py:24
  45.2 13.6 %collective-permute-start.1 = (bf16[2,48,1024]{2,1,0:T(8,128)(2,1)S(1)}, bf16[2,48,1024]{2,1,0:T(8,128)(2,1)S(1)}, u32[]{:S(2)}, u32[]{:S(2)}) collective-permute-start(bf16[2,48,1024]{2,1,0:T(8,128)(2,1)S(1)} %pad_maximum_fusion.3), channel_id=1, source_target_pairs={{0,32},{16,48},{32,0},{48,16},{64,96},{80,112},{96,64},{112,80},{1... | collective-permute-start | bytes 589832 | tf_op jit(solution)/shard_map/ppermute | solution.py:36
  58.9 9.7 %collective-permute-start.6 = (bf16[4,48,1024]{2,1,0:T(8,128)(2,1)S(1)}, bf16[4,48,1024]{2,1,0:T(8,128)(2,1)S(1)}, u32[]{:S(2)}, u32[]{:S(2)}) collective-permute-start(bf16[4,48,1024]{2,1,0:T(8,128)(2,1)S(1)} %pad_maximum_fusion), channel_id=1, source_target_pairs={{0,16},{16,0},{32,48},{48,32},{64,80},{80,64},{96,112},{112,96},{1... | collective-permute-start | bytes 1179656 | tf_op jit(solution)/shard_map/ppermute | solution.py:36
  60.8 14.1 %collective-permute-start.2 = (bf16[192,1024]{1,0:T(8,128)(2,1)S(1)}, bf16[192,1024]{1,0:T(8,128)(2,1)S(1)}, u32[]{:S(2)}, u32[]{:S(2)}) collective-permute-start(bf16[192,1024]{1,0:T(8,128)(2,1)S(1)} %bitcast.29), channel_id=1, source_target_pairs={{128,0},{256,128},{384,256},{0,384},{129,1},{257,129},{385,257},{1... | collective-permute-start | bytes 1179656 | tf_op jit(solution)/shard_map/ppermute | solution.py:32
  63.4 14.0 %collective-permute-start.3 = (bf16[192,1024]{1,0:T(8,128)(2,1)S(1)}, bf16[192,1024]{1,0:T(8,128)(2,1)S(1)}, u32[]{:S(2)}, u32[]{:S(2)}) collective-permute-start(bf16[192,1024]{1,0:T(8,128)(2,1)S(1)} %bitcast.30), channel_id=1, source_target_pairs={{384,0},{0,128},{128,256},{256,384},{385,1},{1,129},{129,257},{257... | collective-permute-start | bytes 1179656 | tf_op jit(solution)/shard_map/ppermute | solution.py:32
  68.5 16.1 %collective-permute-start.8 = (bf16[192,1024]{1,0:T(8,128)(2,1)S(1)}, bf16[192,1024]{1,0:T(8,128)(2,1)S(1)}, u32[]{:S(2)}, u32[]{:S(2)}) collective-permute-start(bf16[192,1024]{1,0:T(8,128)(2,1)S(1)} %bitcast.37), channel_id=1, source_target_pairs={{384,0},{0,128},{128,256},{256,384},{385,1},{1,129},{129,257},{257... | collective-permute-start | bytes 1179656 | tf_op jit(solution)/shard_map/ppermute | solution.py:32
  72.9 17.8 %collective-permute-start.7 = (bf16[192,1024]{1,0:T(8,128)(2,1)S(1)}, bf16[192,1024]{1,0:T(8,128)(2,1)S(1)}, u32[]{:S(2)}, u32[]{:S(2)}) collective-permute-start(bf16[192,1024]{1,0:T(8,128)(2,1)S(1)} %bitcast.38), channel_id=1, source_target_pairs={{128,0},{256,128},{384,256},{0,384},{129,1},{257,129},{385,257},{1... | collective-permute-start | bytes 1179656 | tf_op jit(solution)/shard_map/ppermute | solution.py:32
  74.9 18.7 %collective-permute-start.4 = (bf16[96,1024]{1,0:T(8,128)(2,1)S(1)}, bf16[96,1024]{1,0:T(8,128)(2,1)S(1)}, u32[]{:S(2)}, u32[]{:S(2)}) collective-permute-start(bf16[96,1024]{1,0:T(8,128)(2,1)S(1)} %slice.101), channel_id=1, source_target_pairs={{128,0},{256,128},{384,256},{0,384},{129,1},{257,129},{385,257},{1... | collective-permute-start | bytes 589832 | tf_op jit(solution)/shard_map/ppermute | solution.py:32
  78.1 15.5 %collective-permute-start.5 = (bf16[96,1024]{1,0:T(8,128)(2,1)}, bf16[96,1024]{1,0:T(8,128)(2,1)S(1)}, u32[]{:S(2)}, u32[]{:S(2)}) collective-permute-start(bf16[96,1024]{1,0:T(8,128)(2,1)} %slice.102), channel_id=1, source_target_pairs={{384,0},{0,128},{128,256},{256,384},{385,1},{1,129},{129,257},{257... | collective-permute-start | bytes 589832 | tf_op jit(solution)/shard_map/ppermute | solution.py:32
  85.4 8.8 %collective-permute-start.10 = (bf16[96,1024]{1,0:T(8,128)(2,1)}, bf16[96,1024]{1,0:T(8,128)(2,1)S(1)}, u32[]{:S(2)}, u32[]{:S(2)}) collective-permute-start(bf16[96,1024]{1,0:T(8,128)(2,1)} %slice.104), channel_id=1, source_target_pairs={{384,0},{0,128},{128,256},{256,384},{385,1},{1,129},{129,257},{257... | collective-permute-start | bytes 589832 | tf_op jit(solution)/shard_map/ppermute | solution.py:32
  91.5 9.0 %collective-permute-start.9 = (bf16[96,1024]{1,0:T(8,128)(2,1)}, bf16[96,1024]{1,0:T(8,128)(2,1)S(1)}, u32[]{:S(2)}, u32[]{:S(2)}) collective-permute-start(bf16[96,1024]{1,0:T(8,128)(2,1)} %slice.103), channel_id=1, source_target_pairs={{128,0},{256,128},{384,256},{0,384},{129,1},{257,129},{385,257},{1... | collective-permute-start | bytes 589832 | tf_op jit(solution)/shard_map/ppermute | solution.py:32
  108.6 13.3 %collective-permute-start.11 = (f32[24,1024]{1,0:T(8,128)S(1)}, f32[24,1024]{1,0:T(8,128)S(1)}, u32[]{:S(2)}, u32[]{:S(2)}) collective-permute-start(f32[24,1024]{1,0:T(8,128)S(1)} %get-tuple-element.28), channel_id=1, source_target_pairs={{12,0},{0,4},{4,8},{8,12},{13,1},{1,5},{5,9},{9,13},{14,2},{2,6},{... | collective-permute-start | bytes 294920 | tf_op jit(solution)/shard_map/ppermute | solution.py:32
  111.0 11.0 %collective-permute-start.12 = (f32[24,1024]{1,0:T(8,128)S(1)}, f32[24,1024]{1,0:T(8,128)S(1)}, u32[]{:S(2)}, u32[]{:S(2)}) collective-permute-start(f32[24,1024]{1,0:T(8,128)S(1)} %get-tuple-element.27), channel_id=1, source_target_pairs={{8,0},{12,4},{0,8},{4,12},{9,1},{13,5},{1,9},{5,13},{10,2},{14,6},... | collective-permute-start | bytes 294920 | tf_op jit(solution)/shard_map/ppermute | solution.py:32
  115.1 7.6 %collective-permute-start.13 = (f32[24,1024]{1,0:T(8,128)S(1)}, f32[24,1024]{1,0:T(8,128)S(1)}, u32[]{:S(2)}, u32[]{:S(2)}) collective-permute-start(f32[24,1024]{1,0:T(8,128)S(1)} %get-tuple-element.26), channel_id=1, source_target_pairs={{4,0},{8,4},{12,8},{0,12},{5,1},{9,5},{13,9},{1,13},{6,2},{10,6},{... | collective-permute-start | bytes 294920 | tf_op jit(solution)/shard_map/ppermute | solution.py:32
  117.7 5.1 %copy-start.3 = (bf16[16,8,1024]{2,1,0:T(8,128)(2,1)S(1)}, bf16[16,8,1024]{2,1,0:T(8,128)(2,1)}, u32[]{:S(2)}) copy-start(bf16[16,8,1024]{2,1,0:T(8,128)(2,1)} %param.11) | copy-start | bytes 786436
  117.7 28.0 %all-to-all-start.3 = ((bf16[4,256,1024]{2,1,0:T(8,128)(2,1)}), bf16[4,256,1024]{2,1,0:T(8,128)(2,1)S(1)}, u32[]{:S(2)}, u32[]{:S(2)}) async-start(bf16[4,256,1024]{2,1,0:T(8,128)(2,1)} %get-tuple-element.15), calls=%async_computation.3 | async-start | bytes 4194304 | tf_op jit(solution)/shard_map/all_to_all | solution.py:24
  122.0 23.0 %copy-start.4 = (f32[16,1024]{1,0:T(8,128)S(1)}, f32[16,1024]{1,0:T(8,128)}, u32[]{:S(2)}) copy-start(f32[16,1024]{1,0:T(8,128)} %param.13) | copy-start | bytes 196612
Sparse Core Ops, SparseCore 0:
  12.7 56.2 all-gather.1

commit v4 on v3

--- a/solution.py
+++ b/solution.py
@@ -98,7 +98,7 @@
             jax.ShapeDtypeStruct((rows + EXTRA, depth), BF16),
             jax.ShapeDtypeStruct((NX, own_rows + 4, cols), BF16),
         ),
-        compiler_params=params(),
+        compiler_params=pltpu.CompilerParams(vmem_limit_bytes=60 * 1024 * 1024),
         cost_estimate=cost(4 * rows * depth, 4 * rows * depth),
     )(duals, active.T, weights[None], recourse)
 

time: 155 us -> 155 us (level)
  local copies, waits for them, and re-layouts: 8.51 us -> 6.63 us
    unnamed x14 -> x8, local copies, waits for them, and re-layouts: 4.78 us -> 2.92 us
where the time goes in v4:
time: 155 us; the launch traced here: 153 us
  starting transfers between devices  68.4 us (44%)
  blocking collectives  30.6 us (20%)
  waiting for transfers between devices  19 us (12%)
  between operations  14.4 us (9%)
  Pallas kernels  11.3 us (7%)
  local copies, waits for them, and re-layouts  6.63 us (4%)
  other arithmetic  3.09 us (2%)
    ppermute x11, starting transfers between devices, shift(): lax.ppermute(value, axis, [((i + step) % count, i) for i in range(count)])  37.4 us
    psum x1, blocking collectives, local(): total_sq = lax.psum(squares, DEC)  20.3 us
    all_to_all x3, starting transfers between devices, exchange(): return lax.all_to_all(value, axes, 0, 0, tiled=True)  18.8 us
    ppermute x3, starting transfers between devices, flip(): lax.ppermute(value, ('zq', 'zr'), [(i, i ^ distance) for i in range(NZ)])  12.1 us
    all_to_all x1, blocking collectives, exchange(): return lax.all_to_all(value, axes, 0, 0, tiled=True)  10.3 us
    ppermute x3, waiting for transfers between devices, flip(): lax.ppermute(value, ('zq', 'zr'), [(i, i ^ distance) for i in range(NZ)])  10.2 us
    ppermute x11, waiting for transfers between devices, shift(): lax.ppermute(value, axis, [((i + step) % count, i) for i in range(count)])  8.84 us
    pallas_call x1, Pallas kernels, products(): pl.pallas_call(products_body, grid=(steps,), in_specs=[pl.BlockSpec(memor...  8.18 us
  transfers between devices with their start and end apart: 18, of which 8 were waited for; matrix products, arithmetic and copies ran while one was open for 4% of the time, Pallas kernels for 0%

profile of v4, /device:TPU:24, one launch (start us, length us, event | category | flops | bytes accessed | tf_op | source)
XLA Modules:
  0.0 153.4 jit_solution(1981771583193710776)
XLA Ops:
  7.2 0.0 copy-start.2
  7.2 0.0 all-gather.2.cloned.1.call-start
  7.2 1.6 %copy.18.recourse_ref = bf16[4,12,1024]{2,1,0:T(8,128)(2,1)} copy(bf16[4,12,1024]{2,0,1:T(4,128)(2,1)} %param.8) | data formatting | bytes 196608 | tf_op args[1]
  8.8 3.1 %shard_map.102 = (bf16[304,1536]{1,0:T(8,128)(2,1)}, bf16[4,16,1024]{2,1,0:T(8,128)(2,1)}) custom-call(bf16[256,1536]{1,0:T(8,128)(2,1)} %duals_ref.1, s32[12,256]{1,0:T(8,128)} %bitcast.41, f32[1,256]{1,0:T(1,128)} %bitcast.42, bf16[4,12,1024]{2,1,0:T(8,128)(2,1)} %copy.18.recourse_ref), custom_call_target="tpu_custom_call" | custom-call | flops 1572864 | bytes 1572864 | tf_op jit(solution)/shard_map/pallas_call | solution.py:95
  11.9 0.0 all-gather.2.cloned.1.call-update
  11.9 10.3 %all_to_all.20.got_ref = bf16[4,16,1024]{2,1,0:T(8,128)(2,1)S(1)} all-to-all(bf16[4,16,1024]{2,1,0:T(8,128)(2,1)} %get-tuple-element.10), channel_id=1, replica_groups=mesh['y'=4,'zq'=2,'zr'=4,'x'=4,'zh'=2,'c'=2] {'x'}, dimensions={0} | all-to-all | bytes 262144 | tf_op jit(solution)/shard_map/all_to_all | solution.py:24
  22.2 0.6 broadcast_in_dim.84
  22.9 7.8 %all-to-all-start.1 = ((f32[4,1,1664]{2,1,0:T(1,128)}), f32[4,1,1664]{2,1,0:T(1,128)S(1)}, u32[]{:S(2)}, u32[]{:S(2)}) async-start(f32[4,1,1664]{2,1,0:T(1,128)} %broadcast_in_dim.84), calls=%async_computation.1 | async-start | bytes 53248 | tf_op jit(solution)/shard_map/all_to_all | solution.py:24
  30.7 5.9 %collective-permute-start = (bf16[1,48,1024]{2,1,0:T(8,128)(2,1)S(1)}, bf16[1,48,1024]{2,1,0:T(8,128)(2,1)S(1)}, u32[]{:S(2)}, u32[]{:S(2)}) collective-permute-start(bf16[1,48,1024]{2,1,0:T(8,128)(2,1)S(1)} %bitcast.32), channel_id=1, source_target_pairs={{0,64},{16,80},{32,96},{48,112},{64,0},{80,16},{96,32},{112,48},{1... | collective-permute-start | bytes 294920 | tf_op jit(solution)/shard_map/ppermute | solution.py:36
  36.6 0.0 all-to-all-done.1
  36.7 0.7 broadcast_in_dim.85
  37.4 6.8 %all-to-all-start.2 = ((f32[8,2,1664]{2,1,0:T(2,128)}), f32[8,2,1664]{2,1,0:T(2,128)S(1)}, u32[]{:S(2)}, u32[]{:S(2)}) async-start(f32[8,2,1664]{2,1,0:T(2,128)} %broadcast_in_dim.85), calls=%async_computation.2 | async-start | bytes 212992 | tf_op jit(solution)/shard_map/all_to_all | solution.py:24
  44.2 0.6 collective-permute-done
  44.8 4.2 %collective-permute-start.1 = (bf16[2,48,1024]{2,1,0:T(8,128)(2,1)S(1)}, bf16[2,48,1024]{2,1,0:T(8,128)(2,1)S(1)}, u32[]{:S(2)}, u32[]{:S(2)}) collective-permute-start(bf16[2,48,1024]{2,1,0:T(8,128)(2,1)S(1)} %pad_maximum_fusion.3), channel_id=1, source_target_pairs={{0,32},{16,48},{32,0},{48,16},{64,96},{80,112},{96,64},{112,80},{1... | collective-permute-start | bytes 589832 | tf_op jit(solution)/shard_map/ppermute | solution.py:36
  49.0 0.0 copy-done.2
  49.0 0.1 iota_compare_fusion.1
  49.1 9.3 %collective-permute-done.1 = bf16[2,48,1024]{2,1,0:T(8,128)(2,1)S(1)} collective-permute-done((bf16[2,48,1024]{2,1,0:T(8,128)(2,1)S(1)}, bf16[2,48,1024]{2,1,0:T(8,128)(2,1)S(1)}, u32[]{:S(2)}, u32[]{:S(2)}) %collective-permute-start.1) | collective-permute-done | bytes 196640 | tf_op jit(solution)/shard_map/ppermute | solution.py:36
  58.4 1.9 %collective-permute-start.6 = (bf16[4,48,1024]{2,1,0:T(8,128)(2,1)S(1)}, bf16[4,48,1024]{2,1,0:T(8,128)(2,1)S(1)}, u32[]{:S(2)}, u32[]{:S(2)}) collective-permute-start(bf16[4,48,1024]{2,1,0:T(8,128)(2,1)S(1)} %pad_maximum_fusion), channel_id=1, source_target_pairs={{0,16},{16,0},{32,48},{48,32},{64,80},{80,64},{96,112},{112,96},{1... | collective-permute-start | bytes 1179656 | tf_op jit(solution)/shard_map/ppermute | solution.py:36
  60.3 2.6 %collective-permute-start.2 = (bf16[192,1024]{1,0:T(8,128)(2,1)S(1)}, bf16[192,1024]{1,0:T(8,128)(2,1)S(1)}, u32[]{:S(2)}, u32[]{:S(2)}) collective-permute-start(bf16[192,1024]{1,0:T(8,128)(2,1)S(1)} %bitcast.29), channel_id=1, source_target_pairs={{128,0},{256,128},{384,256},{0,384},{129,1},{257,129},{385,257},{1... | collective-permute-start | bytes 1179656 | tf_op jit(solution)/shard_map/ppermute | solution.py:32
  63.0 4.4 %collective-permute-start.3 = (bf16[192,1024]{1,0:T(8,128)(2,1)S(1)}, bf16[192,1024]{1,0:T(8,128)(2,1)S(1)}, u32[]{:S(2)}, u32[]{:S(2)}) collective-permute-start(bf16[192,1024]{1,0:T(8,128)(2,1)S(1)} %bitcast.30), channel_id=1, source_target_pairs={{384,0},{0,128},{128,256},{256,384},{385,1},{1,129},{129,257},{257... | collective-permute-start | bytes 1179656 | tf_op jit(solution)/shard_map/ppermute | solution.py:32
  67.4 0.0 all-to-all-done.2
  67.5 0.1 fusion.3
  67.7 0.1 fusion.2
  67.7 0.3 collective-permute-done.6
  68.1 4.4 %collective-permute-start.8 = (bf16[192,1024]{1,0:T(8,128)(2,1)S(1)}, bf16[192,1024]{1,0:T(8,128)(2,1)S(1)}, u32[]{:S(2)}, u32[]{:S(2)}) collective-permute-start(bf16[192,1024]{1,0:T(8,128)(2,1)S(1)} %bitcast.35), channel_id=1, source_target_pairs={{384,0},{0,128},{128,256},{256,384},{385,1},{1,129},{129,257},{257... | collective-permute-start | bytes 1179656 | tf_op jit(solution)/shard_map/ppermute | solution.py:32
  72.5 1.9 %collective-permute-start.7 = (bf16[192,1024]{1,0:T(8,128)(2,1)S(1)}, bf16[192,1024]{1,0:T(8,128)(2,1)S(1)}, u32[]{:S(2)}, u32[]{:S(2)}) collective-permute-start(bf16[192,1024]{1,0:T(8,128)(2,1)S(1)} %bitcast.36), channel_id=1, source_target_pairs={{128,0},{256,128},{384,256},{0,384},{129,1},{257,129},{385,257},{1... | collective-permute-start | bytes 1179656 | tf_op jit(solution)/shard_map/ppermute | solution.py:32
  74.4 0.0 collective-permute-done.2.refs_1_
  74.4 2.1 %collective-permute-start.4 = (bf16[96,1024]{1,0:T(8,128)(2,1)S(1)}, bf16[96,1024]{1,0:T(8,128)(2,1)S(1)}, u32[]{:S(2)}, u32[]{:S(2)}) collective-permute-start(bf16[96,1024]{1,0:T(8,128)(2,1)S(1)} %slice.101), channel_id=1, source_target_pairs={{128,0},{256,128},{384,256},{0,384},{129,1},{257,129},{385,257},{1... | collective-permute-start | bytes 589832 | tf_op jit(solution)/shard_map/ppermute | solution.py:32
  76.6 0.4 collective-permute-done.3.refs_2_
  77.0 0.7 slice.102
  77.6 5.6 %collective-permute-start.5 = (bf16[96,1024]{1,0:T(8,128)(2,1)}, bf16[96,1024]{1,0:T(8,128)(2,1)S(1)}, u32[]{:S(2)}, u32[]{:S(2)}) collective-permute-start(bf16[96,1024]{1,0:T(8,128)(2,1)} %slice.102), channel_id=1, source_target_pairs={{384,0},{0,128},{128,256},{256,384},{385,1},{1,129},{129,257},{257... | collective-permute-start | bytes 589832 | tf_op jit(solution)/shard_map/ppermute | solution.py:32
  83.2 1.0 collective-permute-done.8.refs_7_
  84.2 0.7 slice.104
  84.9 5.4 %collective-permute-start.10 = (bf16[96,1024]{1,0:T(8,128)(2,1)}, bf16[96,1024]{1,0:T(8,128)(2,1)S(1)}, u32[]{:S(2)}, u32[]{:S(2)}) collective-permute-start(bf16[96,1024]{1,0:T(8,128)(2,1)} %slice.104), channel_id=1, source_target_pairs={{384,0},{0,128},{128,256},{256,384},{385,1},{1,129},{129,257},{257... | collective-permute-start | bytes 589832 | tf_op jit(solution)/shard_map/ppermute | solution.py:32
  90.3 0.0 collective-permute-done.7.refs_6_
  90.3 0.7 slice.103
  91.0 1.9 %collective-permute-start.9 = (bf16[96,1024]{1,0:T(8,128)(2,1)}, bf16[96,1024]{1,0:T(8,128)(2,1)S(1)}, u32[]{:S(2)}, u32[]{:S(2)}) collective-permute-start(bf16[96,1024]{1,0:T(8,128)(2,1)} %slice.103), channel_id=1, source_target_pairs={{128,0},{256,128},{384,256},{0,384},{129,1},{257,129},{385,257},{1... | collective-permute-start | bytes 589832 | tf_op jit(solution)/shard_map/ppermute | solution.py:32
  92.9 0.2 concatenate.21.top_ref
  93.2 0.0 collective-permute-done.4.refs_3_
  93.2 0.0 collective-permute-done.5.refs_4_
  93.2 0.6 collective-permute-done.10.refs_9_
  93.8 6.2 %collective-permute-done.9.refs_8_ = bf16[96,1024]{1,0:T(8,128)(2,1)S(1)} collective-permute-done((bf16[96,1024]{1,0:T(8,128)(2,1)}, bf16[96,1024]{1,0:T(8,128)(2,1)S(1)}, u32[]{:S(2)}, u32[]{:S(2)}) %collective-permute-start.9) | collective-permute-done | bytes 196640 | tf_op jit(solution)/shard_map/ppermute | solution.py:32
  100.0 0.0 all-gather.2.cloned.1.call-done.left_ref
  100.0 8.2 %shard_map.104 = (f32[4,24,1024]{2,1,0:T(8,128)S(1)}, bf16[4,256,1024]{2,1,0:T(8,128)(2,1)}) custom-call(s32[1]{0:T(128)} %bitcast.x_ref, s32[1]{0:T(128)} %bitcast.1.y_ref, s32[1]{0:T(128)} %bitcast.2.z_ref, bf16[16,1536]{1,0:T(8,128)(2,1)S(1)} %concatenate.21.top_ref, bf16[1216,1536]{1,0:T(8,128)(2,1)} %all-gather.2.cloned.1.call-done.left_ref, ...), custom_call_target="tpu_custom_call" | custom-call | flops 3825205248 | bytes 10000000 | tf_op jit(solution)/shard_map/pallas_call | solution.py:171
  108.2 2.4 %collective-permute-start.11 = (f32[24,1024]{1,0:T(8,128)S(1)}, f32[24,1024]{1,0:T(8,128)S(1)}, u32[]{:S(2)}, u32[]{:S(2)}) collective-permute-start(f32[24,1024]{1,0:T(8,128)S(1)} %get-tuple-element.28), channel_id=1, source_target_pairs={{12,0},{0,4},{4,8},{8,12},{13,1},{1,5},{5,9},{9,13},{14,2},{2,6},{... | collective-permute-start | bytes 294920 | tf_op jit(solution)/shard_map/ppermute | solution.py:32
  110.5 4.1 %collective-permute-start.12 = (f32[24,1024]{1,0:T(8,128)S(1)}, f32[24,1024]{1,0:T(8,128)S(1)}, u32[]{:S(2)}, u32[]{:S(2)}) collective-permute-start(f32[24,1024]{1,0:T(8,128)S(1)} %get-tuple-element.27), channel_id=1, source_target_pairs={{8,0},{12,4},{0,8},{4,12},{9,1},{13,5},{1,9},{5,13},{10,2},{14,6},... | collective-permute-start | bytes 294920 | tf_op jit(solution)/shard_map/ppermute | solution.py:32
  114.6 2.6 %collective-permute-start.13 = (f32[24,1024]{1,0:T(8,128)S(1)}, f32[24,1024]{1,0:T(8,128)S(1)}, u32[]{:S(2)}, u32[]{:S(2)}) collective-permute-start(f32[24,1024]{1,0:T(8,128)S(1)} %get-tuple-element.26), channel_id=1, source_target_pairs={{4,0},{8,4},{12,8},{0,12},{5,1},{9,5},{13,9},{1,13},{6,2},{10,6},{... | collective-permute-start | bytes 294920 | tf_op jit(solution)/shard_map/ppermute | solution.py:32
  117.3 0.0 copy-start
  117.3 4.2 %all-to-all-start.3 = ((bf16[4,256,1024]{2,1,0:T(8,128)(2,1)}), bf16[4,256,1024]{2,1,0:T(8,128)(2,1)S(1)}, u32[]{:S(2)}, u32[]{:S(2)}) async-start(bf16[4,256,1024]{2,1,0:T(8,128)(2,1)} %get-tuple-element.15), calls=%async_computation.3 | async-start | bytes 4194304 | tf_op jit(solution)/shard_map/all_to_all | solution.py:24
  121.5 0.0 copy-start.1
  121.5 0.0 collective-permute-done.11
  121.5 0.0 collective-permute-done.12
  121.5 0.7 collective-permute-done.13
  122.3 0.0 copy-done
  122.3 0.9 select_reduce_fusion
  123.2 0.2 multiply_reduce_fusion
  123.4 20.3 %psum.7 = f32[16]{0:T(128)S(1)} all-reduce(f32[16]{0:T(128)S(1)} %multiply_reduce_fusion), channel_id=1, replica_groups=mesh['y'=4,'zq'=2,'zr'=4,'x'=4,'zh'=2,'c'=2] {'zh','c'}, use_global_device_ids=true, to_apply=%region_5.6 | all-reduce | flops 16 | bytes 128 | tf_op jit(solution)/shard_map/psum | solution.py:256
  143.8 0.7 pad_maximum_fusion.2
  144.6 0.0 copy-done.1
  144.6 0.7 divide_subtract_fusion
  145.3 0.0 all-to-all-done.3
  145.3 1.3 copy.29
  (23 shorter events, 0.4 us)
Async XLA Ops:
  7.2 41.9 %copy-start.2 = (s32[16]{0:T(128)S(1)}, s32[16]{0:T(128)}, u32[]{:S(2)}) copy-start(s32[16]{0:T(128)} %param.12) | copy-start | bytes 196
  7.2 92.8 %all-gather.2.cloned.1.call-start = ((), (), s32[]{:S(2)}) async-start(), calls=%async_computation.4 | async-start | bytes 4669440 | tf_op jit(solution)/shard_map/all_gather | solution.py:203
  22.9 13.8 %all-to-all-start.1 = ((f32[4,1,1664]{2,1,0:T(1,128)}), f32[4,1,1664]{2,1,0:T(1,128)S(1)}, u32[]{:S(2)}, u32[]{:S(2)}) async-start(f32[4,1,1664]{2,1,0:T(1,128)} %broadcast_in_dim.84), calls=%async_computation.1 | async-start | bytes 53248 | tf_op jit(solution)/shard_map/all_to_all | solution.py:24
  30.7 14.1 %collective-permute-start = (bf16[1,48,1024]{2,1,0:T(8,128)(2,1)S(1)}, bf16[1,48,1024]{2,1,0:T(8,128)(2,1)S(1)}, u32[]{:S(2)}, u32[]{:S(2)}) collective-permute-start(bf16[1,48,1024]{2,1,0:T(8,128)(2,1)S(1)} %bitcast.32), channel_id=1, source_target_pairs={{0,64},{16,80},{32,96},{48,112},{64,0},{80,16},{96,32},{112,48},{1... | collective-permute-start | bytes 294920 | tf_op jit(solution)/shard_map/ppermute | solution.py:36
  37.4 30.0 %all-to-all-start.2 = ((f32[8,2,1664]{2,1,0:T(2,128)}), f32[8,2,1664]{2,1,0:T(2,128)S(1)}, u32[]{:S(2)}, u32[]{:S(2)}) async-start(f32[8,2,1664]{2,1,0:T(2,128)} %broadcast_in_dim.85), calls=%async_computation.2 | async-start | bytes 212992 | tf_op jit(solution)/shard_map/all_to_all | solution.py:24
  44.8 13.6 %collective-permute-start.1 = (bf16[2,48,1024]{2,1,0:T(8,128)(2,1)S(1)}, bf16[2,48,1024]{2,1,0:T(8,128)(2,1)S(1)}, u32[]{:S(2)}, u32[]{:S(2)}) collective-permute-start(bf16[2,48,1024]{2,1,0:T(8,128)(2,1)S(1)} %pad_maximum_fusion.3), channel_id=1, source_target_pairs={{0,32},{16,48},{32,0},{48,16},{64,96},{80,112},{96,64},{112,80},{1... | collective-permute-start | bytes 589832 | tf_op jit(solution)/shard_map/ppermute | solution.py:36
  58.4 9.7 %collective-permute-start.6 = (bf16[4,48,1024]{2,1,0:T(8,128)(2,1)S(1)}, bf16[4,48,1024]{2,1,0:T(8,128)(2,1)S(1)}, u32[]{:S(2)}, u32[]{:S(2)}) collective-permute-start(bf16[4,48,1024]{2,1,0:T(8,128)(2,1)S(1)} %pad_maximum_fusion), channel_id=1, source_target_pairs={{0,16},{16,0},{32,48},{48,32},{64,80},{80,64},{96,112},{112,96},{1... | collective-permute-start | bytes 1179656 | tf_op jit(solution)/shard_map/ppermute | solution.py:36
  60.3 14.1 %collective-permute-start.2 = (bf16[192,1024]{1,0:T(8,128)(2,1)S(1)}, bf16[192,1024]{1,0:T(8,128)(2,1)S(1)}, u32[]{:S(2)}, u32[]{:S(2)}) collective-permute-start(bf16[192,1024]{1,0:T(8,128)(2,1)S(1)} %bitcast.29), channel_id=1, source_target_pairs={{128,0},{256,128},{384,256},{0,384},{129,1},{257,129},{385,257},{1... | collective-permute-start | bytes 1179656 | tf_op jit(solution)/shard_map/ppermute | solution.py:32
  63.0 14.0 %collective-permute-start.3 = (bf16[192,1024]{1,0:T(8,128)(2,1)S(1)}, bf16[192,1024]{1,0:T(8,128)(2,1)S(1)}, u32[]{:S(2)}, u32[]{:S(2)}) collective-permute-start(bf16[192,1024]{1,0:T(8,128)(2,1)S(1)} %bitcast.30), channel_id=1, source_target_pairs={{384,0},{0,128},{128,256},{256,384},{385,1},{1,129},{129,257},{257... | collective-permute-start | bytes 1179656 | tf_op jit(solution)/shard_map/ppermute | solution.py:32
  68.1 16.1 %collective-permute-start.8 = (bf16[192,1024]{1,0:T(8,128)(2,1)S(1)}, bf16[192,1024]{1,0:T(8,128)(2,1)S(1)}, u32[]{:S(2)}, u32[]{:S(2)}) collective-permute-start(bf16[192,1024]{1,0:T(8,128)(2,1)S(1)} %bitcast.35), channel_id=1, source_target_pairs={{384,0},{0,128},{128,256},{256,384},{385,1},{1,129},{129,257},{257... | collective-permute-start | bytes 1179656 | tf_op jit(solution)/shard_map/ppermute | solution.py:32
  72.5 17.8 %collective-permute-start.7 = (bf16[192,1024]{1,0:T(8,128)(2,1)S(1)}, bf16[192,1024]{1,0:T(8,128)(2,1)S(1)}, u32[]{:S(2)}, u32[]{:S(2)}) collective-permute-start(bf16[192,1024]{1,0:T(8,128)(2,1)S(1)} %bitcast.36), channel_id=1, source_target_pairs={{128,0},{256,128},{384,256},{0,384},{129,1},{257,129},{385,257},{1... | collective-permute-start | bytes 1179656 | tf_op jit(solution)/shard_map/ppermute | solution.py:32
  74.4 18.7 %collective-permute-start.4 = (bf16[96,1024]{1,0:T(8,128)(2,1)S(1)}, bf16[96,1024]{1,0:T(8,128)(2,1)S(1)}, u32[]{:S(2)}, u32[]{:S(2)}) collective-permute-start(bf16[96,1024]{1,0:T(8,128)(2,1)S(1)} %slice.101), channel_id=1, source_target_pairs={{128,0},{256,128},{384,256},{0,384},{129,1},{257,129},{385,257},{1... | collective-permute-start | bytes 589832 | tf_op jit(solution)/shard_map/ppermute | solution.py:32
  77.6 15.5 %collective-permute-start.5 = (bf16[96,1024]{1,0:T(8,128)(2,1)}, bf16[96,1024]{1,0:T(8,128)(2,1)S(1)}, u32[]{:S(2)}, u32[]{:S(2)}) collective-permute-start(bf16[96,1024]{1,0:T(8,128)(2,1)} %slice.102), channel_id=1, source_target_pairs={{384,0},{0,128},{128,256},{256,384},{385,1},{1,129},{129,257},{257... | collective-permute-start | bytes 589832 | tf_op jit(solution)/shard_map/ppermute | solution.py:32
  84.9 8.8 %collective-permute-start.10 = (bf16[96,1024]{1,0:T(8,128)(2,1)}, bf16[96,1024]{1,0:T(8,128)(2,1)S(1)}, u32[]{:S(2)}, u32[]{:S(2)}) collective-permute-start(bf16[96,1024]{1,0:T(8,128)(2,1)} %slice.104), channel_id=1, source_target_pairs={{384,0},{0,128},{128,256},{256,384},{385,1},{1,129},{129,257},{257... | collective-permute-start | bytes 589832 | tf_op jit(solution)/shard_map/ppermute | solution.py:32
  91.0 9.0 %collective-permute-start.9 = (bf16[96,1024]{1,0:T(8,128)(2,1)}, bf16[96,1024]{1,0:T(8,128)(2,1)S(1)}, u32[]{:S(2)}, u32[]{:S(2)}) collective-permute-start(bf16[96,1024]{1,0:T(8,128)(2,1)} %slice.103), channel_id=1, source_target_pairs={{128,0},{256,128},{384,256},{0,384},{129,1},{257,129},{385,257},{1... | collective-permute-start | bytes 589832 | tf_op jit(solution)/shard_map/ppermute | solution.py:32
  108.2 13.3 %collective-permute-start.11 = (f32[24,1024]{1,0:T(8,128)S(1)}, f32[24,1024]{1,0:T(8,128)S(1)}, u32[]{:S(2)}, u32[]{:S(2)}) collective-permute-start(f32[24,1024]{1,0:T(8,128)S(1)} %get-tuple-element.28), channel_id=1, source_target_pairs={{12,0},{0,4},{4,8},{8,12},{13,1},{1,5},{5,9},{9,13},{14,2},{2,6},{... | collective-permute-start | bytes 294920 | tf_op jit(solution)/shard_map/ppermute | solution.py:32
  110.5 11.0 %collective-permute-start.12 = (f32[24,1024]{1,0:T(8,128)S(1)}, f32[24,1024]{1,0:T(8,128)S(1)}, u32[]{:S(2)}, u32[]{:S(2)}) collective-permute-start(f32[24,1024]{1,0:T(8,128)S(1)} %get-tuple-element.27), channel_id=1, source_target_pairs={{8,0},{12,4},{0,8},{4,12},{9,1},{13,5},{1,9},{5,13},{10,2},{14,6},... | collective-permute-start | bytes 294920 | tf_op jit(solution)/shard_map/ppermute | solution.py:32
  114.6 7.6 %collective-permute-start.13 = (f32[24,1024]{1,0:T(8,128)S(1)}, f32[24,1024]{1,0:T(8,128)S(1)}, u32[]{:S(2)}, u32[]{:S(2)}) collective-permute-start(f32[24,1024]{1,0:T(8,128)S(1)} %get-tuple-element.26), channel_id=1, source_target_pairs={{4,0},{8,4},{12,8},{0,12},{5,1},{9,5},{13,9},{1,13},{6,2},{10,6},{... | collective-permute-start | bytes 294920 | tf_op jit(solution)/shard_map/ppermute | solution.py:32
  117.3 5.1 %copy-start = (bf16[16,8,1024]{2,1,0:T(8,128)(2,1)S(1)}, bf16[16,8,1024]{2,1,0:T(8,128)(2,1)}, u32[]{:S(2)}) copy-start(bf16[16,8,1024]{2,1,0:T(8,128)(2,1)} %param.11) | copy-start | bytes 786436
  117.3 28.0 %all-to-all-start.3 = ((bf16[4,256,1024]{2,1,0:T(8,128)(2,1)}), bf16[4,256,1024]{2,1,0:T(8,128)(2,1)S(1)}, u32[]{:S(2)}, u32[]{:S(2)}) async-start(bf16[4,256,1024]{2,1,0:T(8,128)(2,1)} %get-tuple-element.15), calls=%async_computation.3 | async-start | bytes 4194304 | tf_op jit(solution)/shard_map/all_to_all | solution.py:24
  121.5 23.1 %copy-start.1 = (f32[16,1024]{1,0:T(8,128)S(1)}, f32[16,1024]{1,0:T(8,128)}, u32[]{:S(2)}) copy-start(f32[16,1024]{1,0:T(8,128)} %param.13) | copy-start | bytes 196612
Sparse Core Ops, SparseCore 0:
  12.0 56.2 all-gather.1

commit v5 on v4

--- a/solution.py
+++ b/solution.py
@@ -167,7 +167,8 @@
     cols = pieces[0].shape[1]
     steps = 2
     wide = cols // steps
-    whole = lambda value: pl.BlockSpec(value.shape, lambda j: (0, 0))
+    once = pl.Buffered(1)
+    whole = lambda value: pl.BlockSpec(value.shape, lambda j: (0, 0), pipeline_mode=once)
     return pl.pallas_call(
         products_body,
         grid=(steps,),
@@ -183,7 +184,7 @@
             jax.ShapeDtypeStruct((NX, rows, cols), BF16),
         ),
         scratch_shapes=[pltpu.VMEM((depth, wide), BF16)],
-        compiler_params=params(),
+        compiler_params=pltpu.CompilerParams(vmem_limit_bytes=30 * 1024 * 1024),
         cost_estimate=cost(2 * NX * (rows + EXTRA) * depth * cols, 10_000_000),
     )(x_at, y_at, z_at, top, left, *pieces)
 

time: 155 us -> 155 us (level)
  local copies, waits for them, and re-layouts: 6.63 us -> 8.7 us
  Pallas kernels: 11.3 us -> 9.38 us
    unnamed x8 -> x10, local copies, waits for them, and re-layouts: 2.92 us -> 4.97 us
    pallas_call x1, Pallas kernels: 8.18 us -> 6.29 us  [products(): pl.pallas_call(products_body, grid=(steps,), in_specs=[pl.BlockSpec(memor...]
where the time goes in v5:
time: 155 us; the launch traced here: 154 us
  starting transfers between devices  68.4 us (44%)
  blocking collectives  30.6 us (20%)
  waiting for transfers between devices  19 us (12%)
  between operations  14.4 us (9%)
  Pallas kernels  9.38 us (6%)
  local copies, waits for them, and re-layouts  8.7 us (6%)
  other arithmetic  3.09 us (2%)
    ppermute x11, starting transfers between devices, shift(): lax.ppermute(value, axis, [((i + step) % count, i) for i in range(count)])  37.4 us
    psum x1, blocking collectives, local(): total_sq = lax.psum(squares, DEC)  20.3 us
    all_to_all x3, starting transfers between devices, exchange(): return lax.all_to_all(value, axes, 0, 0, tiled=True)  18.8 us
    ppermute x3, starting transfers between devices, flip(): lax.ppermute(value, ('zq', 'zr'), [(i, i ^ distance) for i in range(NZ)])  12.1 us
    all_to_all x1, blocking collectives, exchange(): return lax.all_to_all(value, axes, 0, 0, tiled=True)  10.3 us
    ppermute x3, waiting for transfers between devices, flip(): lax.ppermute(value, ('zq', 'zr'), [(i, i ^ distance) for i in range(NZ)])  10.2 us
    ppermute x11, waiting for transfers between devices, shift(): lax.ppermute(value, axis, [((i + step) % count, i) for i in range(count)])  8.84 us
    pallas_call x1, Pallas kernels, products(): pl.pallas_call(products_body, grid=(steps,), in_specs=[pl.BlockSpec(memor...  6.29 us
  transfers between devices with their start and end apart: 18, of which 8 were waited for; matrix products, arithmetic and copies ran while one was open for 4% of the time, Pallas kernels for 0%

profile of v5, /device:TPU:24, one launch (start us, length us, event | category | flops | bytes accessed | tf_op | source)
XLA Modules:
  0.0 153.6 jit_solution(15059895788808827866)
XLA Ops:
  7.2 0.0 copy-start.3
  7.2 0.0 all-gather.2.cloned.1.call-start
  7.2 1.6 %copy.18.recourse_ref = bf16[4,12,1024]{2,1,0:T(8,128)(2,1)} copy(bf16[4,12,1024]{2,0,1:T(4,128)(2,1)} %param.8) | data formatting | bytes 196608 | tf_op args[1]
  8.8 3.1 %shard_map.102 = (bf16[304,1536]{1,0:T(8,128)(2,1)}, bf16[4,16,1024]{2,1,0:T(8,128)(2,1)}) custom-call(bf16[256,1536]{1,0:T(8,128)(2,1)} %duals_ref.1, s32[12,256]{1,0:T(8,128)} %bitcast.41, f32[1,256]{1,0:T(1,128)} %bitcast.42, bf16[4,12,1024]{2,1,0:T(8,128)(2,1)} %copy.18.recourse_ref), custom_call_target="tpu_custom_call" | custom-call | flops 1572864 | bytes 1572864 | tf_op jit(solution)/shard_map/pallas_call | solution.py:95
  11.9 0.0 all-gather.2.cloned.1.call-update
  11.9 10.3 %all_to_all.20.got_ref = bf16[4,16,1024]{2,1,0:T(8,128)(2,1)S(1)} all-to-all(bf16[4,16,1024]{2,1,0:T(8,128)(2,1)} %get-tuple-element.10), channel_id=1, replica_groups=mesh['y'=4,'zq'=2,'zr'=4,'x'=4,'zh'=2,'c'=2] {'x'}, dimensions={0} | all-to-all | bytes 262144 | tf_op jit(solution)/shard_map/all_to_all | solution.py:24
  22.2 0.6 broadcast_in_dim.84
  22.9 7.8 %all-to-all-start.1 = ((f32[4,1,1664]{2,1,0:T(1,128)}), f32[4,1,1664]{2,1,0:T(1,128)S(1)}, u32[]{:S(2)}, u32[]{:S(2)}) async-start(f32[4,1,1664]{2,1,0:T(1,128)} %broadcast_in_dim.84), calls=%async_computation.1 | async-start | bytes 53248 | tf_op jit(solution)/shard_map/all_to_all | solution.py:24
  30.7 5.9 %collective-permute-start = (bf16[1,48,1024]{2,1,0:T(8,128)(2,1)S(1)}, bf16[1,48,1024]{2,1,0:T(8,128)(2,1)S(1)}, u32[]{:S(2)}, u32[]{:S(2)}) collective-permute-start(bf16[1,48,1024]{2,1,0:T(8,128)(2,1)S(1)} %bitcast.32), channel_id=1, source_target_pairs={{0,64},{16,80},{32,96},{48,112},{64,0},{80,16},{96,32},{112,48},{1... | collective-permute-start | bytes 294920 | tf_op jit(solution)/shard_map/ppermute | solution.py:36
  36.6 0.0 all-to-all-done.1
  36.7 0.7 broadcast_in_dim.85
  37.4 6.8 %all-to-all-start.2 = ((f32[8,2,1664]{2,1,0:T(2,128)}), f32[8,2,1664]{2,1,0:T(2,128)S(1)}, u32[]{:S(2)}, u32[]{:S(2)}) async-start(f32[8,2,1664]{2,1,0:T(2,128)} %broadcast_in_dim.85), calls=%async_computation.2 | async-start | bytes 212992 | tf_op jit(solution)/shard_map/all_to_all | solution.py:24
  44.2 0.6 collective-permute-done
  44.8 4.2 %collective-permute-start.1 = (bf16[2,48,1024]{2,1,0:T(8,128)(2,1)S(1)}, bf16[2,48,1024]{2,1,0:T(8,128)(2,1)S(1)}, u32[]{:S(2)}, u32[]{:S(2)}) collective-permute-start(bf16[2,48,1024]{2,1,0:T(8,128)(2,1)S(1)} %pad_maximum_fusion.3), channel_id=1, source_target_pairs={{0,32},{16,48},{32,0},{48,16},{64,96},{80,112},{96,64},{112,80},{1... | collective-permute-start | bytes 589832 | tf_op jit(solution)/shard_map/ppermute | solution.py:36
  49.0 0.0 copy-done.3
  49.0 0.1 iota_compare_fusion.1
  49.1 9.3 %collective-permute-done.1 = bf16[2,48,1024]{2,1,0:T(8,128)(2,1)S(1)} collective-permute-done((bf16[2,48,1024]{2,1,0:T(8,128)(2,1)S(1)}, bf16[2,48,1024]{2,1,0:T(8,128)(2,1)S(1)}, u32[]{:S(2)}, u32[]{:S(2)}) %collective-permute-start.1) | collective-permute-done | bytes 196640 | tf_op jit(solution)/shard_map/ppermute | solution.py:36
  58.4 1.9 %collective-permute-start.6 = (bf16[4,48,1024]{2,1,0:T(8,128)(2,1)S(1)}, bf16[4,48,1024]{2,1,0:T(8,128)(2,1)S(1)}, u32[]{:S(2)}, u32[]{:S(2)}) collective-permute-start(bf16[4,48,1024]{2,1,0:T(8,128)(2,1)S(1)} %pad_maximum_fusion), channel_id=1, source_target_pairs={{0,16},{16,0},{32,48},{48,32},{64,80},{80,64},{96,112},{112,96},{1... | collective-permute-start | bytes 1179656 | tf_op jit(solution)/shard_map/ppermute | solution.py:36
  60.3 2.6 %collective-permute-start.2 = (bf16[192,1024]{1,0:T(8,128)(2,1)S(1)}, bf16[192,1024]{1,0:T(8,128)(2,1)S(1)}, u32[]{:S(2)}, u32[]{:S(2)}) collective-permute-start(bf16[192,1024]{1,0:T(8,128)(2,1)S(1)} %bitcast.29), channel_id=1, source_target_pairs={{128,0},{256,128},{384,256},{0,384},{129,1},{257,129},{385,257},{1... | collective-permute-start | bytes 1179656 | tf_op jit(solution)/shard_map/ppermute | solution.py:32
  63.0 4.4 %collective-permute-start.3 = (bf16[192,1024]{1,0:T(8,128)(2,1)S(1)}, bf16[192,1024]{1,0:T(8,128)(2,1)S(1)}, u32[]{:S(2)}, u32[]{:S(2)}) collective-permute-start(bf16[192,1024]{1,0:T(8,128)(2,1)S(1)} %bitcast.30), channel_id=1, source_target_pairs={{384,0},{0,128},{128,256},{256,384},{385,1},{1,129},{129,257},{257... | collective-permute-start | bytes 1179656 | tf_op jit(solution)/shard_map/ppermute | solution.py:32
  67.4 0.0 all-to-all-done.2
  67.5 0.1 fusion.3
  67.7 0.1 fusion.2
  67.7 0.3 collective-permute-done.6
  68.1 4.4 %collective-permute-start.8 = (bf16[192,1024]{1,0:T(8,128)(2,1)S(1)}, bf16[192,1024]{1,0:T(8,128)(2,1)S(1)}, u32[]{:S(2)}, u32[]{:S(2)}) collective-permute-start(bf16[192,1024]{1,0:T(8,128)(2,1)S(1)} %bitcast.35), channel_id=1, source_target_pairs={{384,0},{0,128},{128,256},{256,384},{385,1},{1,129},{129,257},{257... | collective-permute-start | bytes 1179656 | tf_op jit(solution)/shard_map/ppermute | solution.py:32
  72.5 1.9 %collective-permute-start.7 = (bf16[192,1024]{1,0:T(8,128)(2,1)S(1)}, bf16[192,1024]{1,0:T(8,128)(2,1)S(1)}, u32[]{:S(2)}, u32[]{:S(2)}) collective-permute-start(bf16[192,1024]{1,0:T(8,128)(2,1)S(1)} %bitcast.36), channel_id=1, source_target_pairs={{128,0},{256,128},{384,256},{0,384},{129,1},{257,129},{385,257},{1... | collective-permute-start | bytes 1179656 | tf_op jit(solution)/shard_map/ppermute | solution.py:32
  74.4 0.0 collective-permute-done.2.refs_1_
  74.4 2.1 %collective-permute-start.4 = (bf16[96,1024]{1,0:T(8,128)(2,1)S(1)}, bf16[96,1024]{1,0:T(8,128)(2,1)S(1)}, u32[]{:S(2)}, u32[]{:S(2)}) collective-permute-start(bf16[96,1024]{1,0:T(8,128)(2,1)S(1)} %slice.101), channel_id=1, source_target_pairs={{128,0},{256,128},{384,256},{0,384},{129,1},{257,129},{385,257},{1... | collective-permute-start | bytes 589832 | tf_op jit(solution)/shard_map/ppermute | solution.py:32
  76.6 0.4 collective-permute-done.3.refs_2_
  77.0 0.7 slice.102
  77.6 5.6 %collective-permute-start.5 = (bf16[96,1024]{1,0:T(8,128)(2,1)}, bf16[96,1024]{1,0:T(8,128)(2,1)S(1)}, u32[]{:S(2)}, u32[]{:S(2)}) collective-permute-start(bf16[96,1024]{1,0:T(8,128)(2,1)} %slice.102), channel_id=1, source_target_pairs={{384,0},{0,128},{128,256},{256,384},{385,1},{1,129},{129,257},{257... | collective-permute-start | bytes 589832 | tf_op jit(solution)/shard_map/ppermute | solution.py:32
  83.2 1.0 collective-permute-done.8.refs_7_
  84.2 0.7 slice.104
  84.9 5.4 %collective-permute-start.10 = (bf16[96,1024]{1,0:T(8,128)(2,1)}, bf16[96,1024]{1,0:T(8,128)(2,1)S(1)}, u32[]{:S(2)}, u32[]{:S(2)}) collective-permute-start(bf16[96,1024]{1,0:T(8,128)(2,1)} %slice.104), channel_id=1, source_target_pairs={{384,0},{0,128},{128,256},{256,384},{385,1},{1,129},{129,257},{257... | collective-permute-start | bytes 589832 | tf_op jit(solution)/shard_map/ppermute | solution.py:32
  90.3 0.0 collective-permute-done.7.refs_6_
  90.3 0.7 slice.103
  91.0 1.9 %collective-permute-start.9 = (bf16[96,1024]{1,0:T(8,128)(2,1)}, bf16[96,1024]{1,0:T(8,128)(2,1)S(1)}, u32[]{:S(2)}, u32[]{:S(2)}) collective-permute-start(bf16[96,1024]{1,0:T(8,128)(2,1)} %slice.103), channel_id=1, source_target_pairs={{128,0},{256,128},{384,256},{0,384},{129,1},{257,129},{385,257},{1... | collective-permute-start | bytes 589832 | tf_op jit(solution)/shard_map/ppermute | solution.py:32
  93.0 0.2 concatenate.21.top_ref
  93.2 0.0 collective-permute-done.4.refs_3_
  93.2 0.0 collective-permute-done.5.refs_4_
  93.2 0.6 collective-permute-done.10.refs_9_
  93.8 6.2 %collective-permute-done.9.refs_8_ = bf16[96,1024]{1,0:T(8,128)(2,1)S(1)} collective-permute-done((bf16[96,1024]{1,0:T(8,128)(2,1)}, bf16[96,1024]{1,0:T(8,128)(2,1)S(1)}, u32[]{:S(2)}, u32[]{:S(2)}) %collective-permute-start.9) | collective-permute-done | bytes 196640 | tf_op jit(solution)/shard_map/ppermute | solution.py:32
  100.0 0.0 all-gather.2.cloned.1.call-done.left_ref
  100.0 0.0 copy-start
  100.0 2.1 %copy-done = bf16[1216,1536]{1,0:T(8,128)(2,1)S(1)} copy-done((bf16[1216,1536]{1,0:T(8,128)(2,1)S(1)}, bf16[1216,1536]{1,0:T(8,128)(2,1)}, u32[]{:S(2)}) %copy-start) | copy-done | bytes 3735576
  102.0 6.3 %shard_map.104 = (f32[4,24,1024]{2,1,0:T(8,128)S(1)}, bf16[4,256,1024]{2,1,0:T(8,128)(2,1)}) custom-call(s32[1]{0:T(128)} %bitcast.x_ref, s32[1]{0:T(128)} %bitcast.1.y_ref, s32[1]{0:T(128)} %bitcast.2.z_ref, bf16[16,1536]{1,0:T(8,128)(2,1)S(1)} %concatenate.21.top_ref, bf16[1216,1536]{1,0:T(8,128)(2,1)S(1)} %copy-done, bf16[192,1024]{1,0:T(8,128)(2,1)S(1)} %bitcast.31, ...), custom_call_target="tpu_custom_call" | custom-call | flops 3825205248 | bytes 10000000 | tf_op jit(solution)/shard_map/pallas_call | solution.py:172
  108.4 2.4 %collective-permute-start.11 = (f32[24,1024]{1,0:T(8,128)S(1)}, f32[24,1024]{1,0:T(8,128)S(1)}, u32[]{:S(2)}, u32[]{:S(2)}) collective-permute-start(f32[24,1024]{1,0:T(8,128)S(1)} %get-tuple-element.28), channel_id=1, source_target_pairs={{12,0},{0,4},{4,8},{8,12},{13,1},{1,5},{5,9},{9,13},{14,2},{2,6},{... | collective-permute-start | bytes 294920 | tf_op jit(solution)/shard_map/ppermute | solution.py:32
  110.7 4.1 %collective-permute-start.12 = (f32[24,1024]{1,0:T(8,128)S(1)}, f32[24,1024]{1,0:T(8,128)S(1)}, u32[]{:S(2)}, u32[]{:S(2)}) collective-permute-start(f32[24,1024]{1,0:T(8,128)S(1)} %get-tuple-element.27), channel_id=1, source_target_pairs={{8,0},{12,4},{0,8},{4,12},{9,1},{13,5},{1,9},{5,13},{10,2},{14,6},... | collective-permute-start | bytes 294920 | tf_op jit(solution)/shard_map/ppermute | solution.py:32
  114.8 2.6 %collective-permute-start.13 = (f32[24,1024]{1,0:T(8,128)S(1)}, f32[24,1024]{1,0:T(8,128)S(1)}, u32[]{:S(2)}, u32[]{:S(2)}) collective-permute-start(f32[24,1024]{1,0:T(8,128)S(1)} %get-tuple-element.26), channel_id=1, source_target_pairs={{4,0},{8,4},{12,8},{0,12},{5,1},{9,5},{13,9},{1,13},{6,2},{10,6},{... | collective-permute-start | bytes 294920 | tf_op jit(solution)/shard_map/ppermute | solution.py:32
  117.4 0.0 copy-start.1
  117.5 4.2 %all-to-all-start.3 = ((bf16[4,256,1024]{2,1,0:T(8,128)(2,1)}), bf16[4,256,1024]{2,1,0:T(8,128)(2,1)S(1)}, u32[]{:S(2)}, u32[]{:S(2)}) async-start(bf16[4,256,1024]{2,1,0:T(8,128)(2,1)} %get-tuple-element.15), calls=%async_computation.3 | async-start | bytes 4194304 | tf_op jit(solution)/shard_map/all_to_all | solution.py:24
  121.7 0.0 copy-start.2
  121.7 0.0 collective-permute-done.11
  121.7 0.0 collective-permute-done.12
  121.7 0.7 collective-permute-done.13
  122.5 0.0 copy-done.1
  122.5 0.9 select_reduce_fusion
  123.4 0.2 multiply_reduce_fusion
  123.6 20.3 %psum.7 = f32[16]{0:T(128)S(1)} all-reduce(f32[16]{0:T(128)S(1)} %multiply_reduce_fusion), channel_id=1, replica_groups=mesh['y'=4,'zq'=2,'zr'=4,'x'=4,'zh'=2,'c'=2] {'zh','c'}, use_global_device_ids=true, to_apply=%region_5.6 | all-reduce | flops 16 | bytes 128 | tf_op jit(solution)/shard_map/psum | solution.py:257
  144.0 0.7 pad_maximum_fusion.2
  144.7 0.0 copy-done.2
  144.7 0.7 divide_subtract_fusion
  145.5 0.0 all-to-all-done.3
  145.5 1.3 copy.29
  (23 shorter events, 0.4 us)
Async XLA Ops:
  7.2 41.9 %copy-start.3 = (s32[16]{0:T(128)S(1)}, s32[16]{0:T(128)}, u32[]{:S(2)}) copy-start(s32[16]{0:T(128)} %param.12) | copy-start | bytes 196
  7.2 92.8 %all-gather.2.cloned.1.call-start = ((), (), s32[]{:S(2)}) async-start(), calls=%async_computation.4 | async-start | bytes 4669440 | tf_op jit(solution)/shard_map/all_gather | solution.py:204
  22.9 13.8 %all-to-all-start.1 = ((f32[4,1,1664]{2,1,0:T(1,128)}), f32[4,1,1664]{2,1,0:T(1,128)S(1)}, u32[]{:S(2)}, u32[]{:S(2)}) async-start(f32[4,1,1664]{2,1,0:T(1,128)} %broadcast_in_dim.84), calls=%async_computation.1 | async-start | bytes 53248 | tf_op jit(solution)/shard_map/all_to_all | solution.py:24
  30.7 14.1 %collective-permute-start = (bf16[1,48,1024]{2,1,0:T(8,128)(2,1)S(1)}, bf16[1,48,1024]{2,1,0:T(8,128)(2,1)S(1)}, u32[]{:S(2)}, u32[]{:S(2)}) collective-permute-start(bf16[1,48,1024]{2,1,0:T(8,128)(2,1)S(1)} %bitcast.32), channel_id=1, source_target_pairs={{0,64},{16,80},{32,96},{48,112},{64,0},{80,16},{96,32},{112,48},{1... | collective-permute-start | bytes 294920 | tf_op jit(solution)/shard_map/ppermute | solution.py:36
  37.4 30.0 %all-to-all-start.2 = ((f32[8,2,1664]{2,1,0:T(2,128)}), f32[8,2,1664]{2,1,0:T(2,128)S(1)}, u32[]{:S(2)}, u32[]{:S(2)}) async-start(f32[8,2,1664]{2,1,0:T(2,128)} %broadcast_in_dim.85), calls=%async_computation.2 | async-start | bytes 212992 | tf_op jit(solution)/shard_map/all_to_all | solution.py:24
  44.8 13.6 %collective-permute-start.1 = (bf16[2,48,1024]{2,1,0:T(8,128)(2,1)S(1)}, bf16[2,48,1024]{2,1,0:T(8,128)(2,1)S(1)}, u32[]{:S(2)}, u32[]{:S(2)}) collective-permute-start(bf16[2,48,1024]{2,1,0:T(8,128)(2,1)S(1)} %pad_maximum_fusion.3), channel_id=1, source_target_pairs={{0,32},{16,48},{32,0},{48,16},{64,96},{80,112},{96,64},{112,80},{1... | collective-permute-start | bytes 589832 | tf_op jit(solution)/shard_map/ppermute | solution.py:36
  58.4 9.7 %collective-permute-start.6 = (bf16[4,48,1024]{2,1,0:T(8,128)(2,1)S(1)}, bf16[4,48,1024]{2,1,0:T(8,128)(2,1)S(1)}, u32[]{:S(2)}, u32[]{:S(2)}) collective-permute-start(bf16[4,48,1024]{2,1,0:T(8,128)(2,1)S(1)} %pad_maximum_fusion), channel_id=1, source_target_pairs={{0,16},{16,0},{32,48},{48,32},{64,80},{80,64},{96,112},{112,96},{1... | collective-permute-start | bytes 1179656 | tf_op jit(solution)/shard_map/ppermute | solution.py:36
  60.3 14.1 %collective-permute-start.2 = (bf16[192,1024]{1,0:T(8,128)(2,1)S(1)}, bf16[192,1024]{1,0:T(8,128)(2,1)S(1)}, u32[]{:S(2)}, u32[]{:S(2)}) collective-permute-start(bf16[192,1024]{1,0:T(8,128)(2,1)S(1)} %bitcast.29), channel_id=1, source_target_pairs={{128,0},{256,128},{384,256},{0,384},{129,1},{257,129},{385,257},{1... | collective-permute-start | bytes 1179656 | tf_op jit(solution)/shard_map/ppermute | solution.py:32
  63.0 14.0 %collective-permute-start.3 = (bf16[192,1024]{1,0:T(8,128)(2,1)S(1)}, bf16[192,1024]{1,0:T(8,128)(2,1)S(1)}, u32[]{:S(2)}, u32[]{:S(2)}) collective-permute-start(bf16[192,1024]{1,0:T(8,128)(2,1)S(1)} %bitcast.30), channel_id=1, source_target_pairs={{384,0},{0,128},{128,256},{256,384},{385,1},{1,129},{129,257},{257... | collective-permute-start | bytes 1179656 | tf_op jit(solution)/shard_map/ppermute | solution.py:32
  68.1 16.1 %collective-permute-start.8 = (bf16[192,1024]{1,0:T(8,128)(2,1)S(1)}, bf16[192,1024]{1,0:T(8,128)(2,1)S(1)}, u32[]{:S(2)}, u32[]{:S(2)}) collective-permute-start(bf16[192,1024]{1,0:T(8,128)(2,1)S(1)} %bitcast.35), channel_id=1, source_target_pairs={{384,0},{0,128},{128,256},{256,384},{385,1},{1,129},{129,257},{257... | collective-permute-start | bytes 1179656 | tf_op jit(solution)/shard_map/ppermute | solution.py:32
  72.5 17.8 %collective-permute-start.7 = (bf16[192,1024]{1,0:T(8,128)(2,1)S(1)}, bf16[192,1024]{1,0:T(8,128)(2,1)S(1)}, u32[]{:S(2)}, u32[]{:S(2)}) collective-permute-start(bf16[192,1024]{1,0:T(8,128)(2,1)S(1)} %bitcast.36), channel_id=1, source_target_pairs={{128,0},{256,128},{384,256},{0,384},{129,1},{257,129},{385,257},{1... | collective-permute-start | bytes 1179656 | tf_op jit(solution)/shard_map/ppermute | solution.py:32
  74.4 18.7 %collective-permute-start.4 = (bf16[96,1024]{1,0:T(8,128)(2,1)S(1)}, bf16[96,1024]{1,0:T(8,128)(2,1)S(1)}, u32[]{:S(2)}, u32[]{:S(2)}) collective-permute-start(bf16[96,1024]{1,0:T(8,128)(2,1)S(1)} %slice.101), channel_id=1, source_target_pairs={{128,0},{256,128},{384,256},{0,384},{129,1},{257,129},{385,257},{1... | collective-permute-start | bytes 589832 | tf_op jit(solution)/shard_map/ppermute | solution.py:32
  77.6 15.6 %collective-permute-start.5 = (bf16[96,1024]{1,0:T(8,128)(2,1)}, bf16[96,1024]{1,0:T(8,128)(2,1)S(1)}, u32[]{:S(2)}, u32[]{:S(2)}) collective-permute-start(bf16[96,1024]{1,0:T(8,128)(2,1)} %slice.102), channel_id=1, source_target_pairs={{384,0},{0,128},{128,256},{256,384},{385,1},{1,129},{129,257},{257... | collective-permute-start | bytes 589832 | tf_op jit(solution)/shard_map/ppermute | solution.py:32
  84.9 8.8 %collective-permute-start.10 = (bf16[96,1024]{1,0:T(8,128)(2,1)}, bf16[96,1024]{1,0:T(8,128)(2,1)S(1)}, u32[]{:S(2)}, u32[]{:S(2)}) collective-permute-start(bf16[96,1024]{1,0:T(8,128)(2,1)} %slice.104), channel_id=1, source_target_pairs={{384,0},{0,128},{128,256},{256,384},{385,1},{1,129},{129,257},{257... | collective-permute-start | bytes 589832 | tf_op jit(solution)/shard_map/ppermute | solution.py:32
  91.0 9.0 %collective-permute-start.9 = (bf16[96,1024]{1,0:T(8,128)(2,1)}, bf16[96,1024]{1,0:T(8,128)(2,1)S(1)}, u32[]{:S(2)}, u32[]{:S(2)}) collective-permute-start(bf16[96,1024]{1,0:T(8,128)(2,1)} %slice.103), channel_id=1, source_target_pairs={{128,0},{256,128},{384,256},{0,384},{129,1},{257,129},{385,257},{1... | collective-permute-start | bytes 589832 | tf_op jit(solution)/shard_map/ppermute | solution.py:32
  100.0 2.1 %copy-start = (bf16[1216,1536]{1,0:T(8,128)(2,1)S(1)}, bf16[1216,1536]{1,0:T(8,128)(2,1)}, u32[]{:S(2)}) copy-start(bf16[1216,1536]{1,0:T(8,128)(2,1)} %all-gather.2.cloned.1.call-done.left_ref) | copy-start | bytes 11206660
  108.4 13.3 %collective-permute-start.11 = (f32[24,1024]{1,0:T(8,128)S(1)}, f32[24,1024]{1,0:T(8,128)S(1)}, u32[]{:S(2)}, u32[]{:S(2)}) collective-permute-start(f32[24,1024]{1,0:T(8,128)S(1)} %get-tuple-element.28), channel_id=1, source_target_pairs={{12,0},{0,4},{4,8},{8,12},{13,1},{1,5},{5,9},{9,13},{14,2},{2,6},{... | collective-permute-start | bytes 294920 | tf_op jit(solution)/shard_map/ppermute | solution.py:32
  110.7 11.0 %collective-permute-start.12 = (f32[24,1024]{1,0:T(8,128)S(1)}, f32[24,1024]{1,0:T(8,128)S(1)}, u32[]{:S(2)}, u32[]{:S(2)}) collective-permute-start(f32[24,1024]{1,0:T(8,128)S(1)} %get-tuple-element.27), channel_id=1, source_target_pairs={{8,0},{12,4},{0,8},{4,12},{9,1},{13,5},{1,9},{5,13},{10,2},{14,6},... | collective-permute-start | bytes 294920 | tf_op jit(solution)/shard_map/ppermute | solution.py:32
  114.8 7.6 %collective-permute-start.13 = (f32[24,1024]{1,0:T(8,128)S(1)}, f32[24,1024]{1,0:T(8,128)S(1)}, u32[]{:S(2)}, u32[]{:S(2)}) collective-permute-start(f32[24,1024]{1,0:T(8,128)S(1)} %get-tuple-element.26), channel_id=1, source_target_pairs={{4,0},{8,4},{12,8},{0,12},{5,1},{9,5},{13,9},{1,13},{6,2},{10,6},{... | collective-permute-start | bytes 294920 | tf_op jit(solution)/shard_map/ppermute | solution.py:32
  117.4 5.1 %copy-start.1 = (bf16[16,8,1024]{2,1,0:T(8,128)(2,1)S(1)}, bf16[16,8,1024]{2,1,0:T(8,128)(2,1)}, u32[]{:S(2)}) copy-start(bf16[16,8,1024]{2,1,0:T(8,128)(2,1)} %param.11) | copy-start | bytes 786436
  117.5 28.0 %all-to-all-start.3 = ((bf16[4,256,1024]{2,1,0:T(8,128)(2,1)}), bf16[4,256,1024]{2,1,0:T(8,128)(2,1)S(1)}, u32[]{:S(2)}, u32[]{:S(2)}) async-start(bf16[4,256,1024]{2,1,0:T(8,128)(2,1)} %get-tuple-element.15), calls=%async_computation.3 | async-start | bytes 4194304 | tf_op jit(solution)/shard_map/all_to_all | solution.py:24
  121.7 23.1 %copy-start.2 = (f32[16,1024]{1,0:T(8,128)S(1)}, f32[16,1024]{1,0:T(8,128)}, u32[]{:S(2)}) copy-start(f32[16,1024]{1,0:T(8,128)} %param.13) | copy-start | bytes 196612
Sparse Core Ops, SparseCore 0:
  12.0 56.2 all-gather.1
